TPU v7x, 256 devices: a whole 4x4x8 slice. The times are simulated.
256 devices in a mesh: role: 4 (over z_lo), tp: 64 (over z_hi, x, y, core).
Axes of the slice: x: 4, y: 4, z: 8 (z_hi: 2, z_lo: 4; z = z_hi * 4 + z_lo), core: 2. Of those that a mesh axis runs over, the one named last changes fastest.
Arguments:
- queries: bfloat16 [32, 16384], P('role'), may hold values from -35 to 35
- cache: bfloat16 [8, 65536, 512], P('role', 'tp'), may hold values from -9 to 9
- beam_sequence: int32 [32], P('role'), may hold values from 0 to 1
- ffn_input: bfloat16 [128, 7168], P('role', 'tp'), may hold values from -6 to 6
- expert_ids: int32 [128, 3], P('role'), may hold values from 0 to 7, all different within a row; in each aligned block of 32 rows (0 to 31, 32 to 63, ...) at most 16 rows name the same one
- route_weights: float32 [128, 3], P('role'), may hold values from 0.2 to 1
- gate_up: bfloat16 [8, 7168, 2, 5120], P('role', None, None, 'tp'), may hold values from -0.0625 to 0.0625
- down_proj: bfloat16 [8, 5120, 7168], P('role', 'tp'), may hold values from -0.078125 to 0.078125
Outputs:
- attention_out: bfloat16 [32, 16384], P('role', 'tp')
- ffn_out: bfloat16 [128, 7168], P('role', 'tp')
Inputs may be any that keep to these rules, and one draw needn't show every extreme that they name: `expert_ids`: each row names 3 different experts. Within the 32 rows of one group (rows g * 32 to (g + 1) * 32 - 1), no expert is named by more than 16 rows, and in some groups one expert is named by exactly 16.
All inputs are finite; a program needn't handle non-finite values.
Results may differ from a plain program's by a relative error of at most 0.013.
Values may be sent and summed in bfloat16 or wider, within the bound.
No kernel may reach another device: no remote copies, remote signals or barrier semaphores. Data moves between devices by JAX's collectives and lax.ppermute only.
A program may use at most 128 MiB of HBM per device.

v0:
```python
import jax
import jax.numpy as jnp
from jax import lax
from jax.sharding import PartitionSpec as P

CAP = 16


def merged(part, axis, combine):
    gathered = jax.tree.map(lambda a: lax.all_gather(a, axis), part)

    def take(source):
        return jax.tree.map(lambda a: lax.dynamic_index_in_dim(a, source, 0, False), gathered)

    return lax.fori_loop(
        1, lax.axis_size(axis), lambda source, state: combine(state, take(source)), take(0)
    )


def masked_scores(queries, cache, beam_sequence):
    rows = queries.shape[0]
    depth = cache.shape[2] // 2
    heads = queries.shape[1] // depth
    query = queries.reshape(rows, heads, depth)
    scores = None
    for seq_local in range(cache.shape[0]):
        part_scores = jnp.einsum(
            "rhd,kd->rhk", query, cache[seq_local, :, :depth], preferred_element_type=jnp.float32
        ) * depth ** (-0.5)
        chosen = (beam_sequence == seq_local)[:, None, None]
        scores = part_scores if scores is None else jnp.where(chosen, part_scores, scores)
    return scores


def weighted_values(scores, top, cache, beam_sequence):
    depth = cache.shape[2] // 2
    expo = jnp.exp(scores - top[:, :, None])
    total = jnp.sum(expo, axis=2)
    rounded = expo.astype(jnp.bfloat16)
    summed = None
    for seq_local in range(cache.shape[0]):
        chosen = (beam_sequence == seq_local)[:, None, None]
        masked = jnp.where(chosen, rounded, jnp.zeros_like(rounded))
        term = jnp.einsum(
            "rhk,kd->rhd", masked, cache[seq_local, :, depth:], preferred_element_type=jnp.float32
        )
        summed = term if summed is None else summed + term
    return (total, summed)


def join_softmax(first, second):
    top = jnp.maximum(first[0], second[0])
    scale_first = jnp.exp(first[0] - top)
    scale_second = jnp.exp(second[0] - top)
    total = first[1] * scale_first + second[1] * scale_second
    summed = first[2] * scale_first[:, :, None] + second[2] * scale_second[:, :, None]
    return (top, total, summed)


def shards(queries, cache, beam_sequence, ffn_input, expert_ids, route_weights, gate_up, down_proj):
    rows_attn = queries.shape[0]
    scores = masked_scores(queries, cache, beam_sequence)
    local_top = jnp.max(scores, axis=2)
    total, summed = weighted_values(scores, local_top, cache, beam_sequence)
    top, total, summed = merged((local_top, total, summed), "tp", join_softmax)
    heads_dev = summed.shape[1] // lax.axis_size("tp")
    start = lax.axis_index("tp") * heads_dev
    mine = lax.dynamic_slice_in_dim(summed / total[:, :, None], start, heads_dev, 1)
    attention_out = mine.reshape(rows_attn, -1).astype(jnp.bfloat16)
    n_role = lax.axis_size("role")
    experts_here = gate_up.shape[0]
    width = ffn_input.shape[1]
    topk = expert_ids.shape[1]
    rows_ffn = ffn_input.shape[0]
    flat = expert_ids.reshape(-1)
    pairs = flat.shape[0]
    n_exp = experts_here * n_role
    hits = (flat[:, None] == jnp.arange(n_exp, dtype=jnp.int32)[None, :]).astype(jnp.int32)
    slot = jnp.sum((jnp.cumsum(hits, axis=0) - hits) * hits, axis=1)
    place = flat % experts_here * (n_role * CAP) + flat // experts_here * CAP + slot
    slots = experts_here * n_role * CAP
    select = place[:, None] == jnp.arange(slots, dtype=jnp.int32)[None, :]
    repeated = jnp.repeat(ffn_input, topk, axis=0)
    send = jnp.einsum(
        "ps,pd->sd", select.astype(jnp.bfloat16), repeated, preferred_element_type=jnp.float32
    ).astype(jnp.bfloat16)
    send = send.reshape(experts_here, n_role, CAP, width)
    received = lax.all_to_all(send, "role", split_axis=1, concat_axis=1, tiled=True)
    received = received.reshape(experts_here, n_role * CAP, width)
    weights_flat = gate_up.reshape(experts_here, gate_up.shape[1], -1)
    units = gate_up.shape[3]
    both = jnp.einsum(
        "erd,edf->erf",
        lax.all_gather(received, "tp", axis=2, tiled=True),
        weights_flat,
        preferred_element_type=jnp.float32,
    )
    hidden = (jax.nn.silu(both[:, :, :units]) * both[:, :, units:]).astype(jnp.bfloat16)
    partial_value = jnp.einsum(
        "erf,efd->der", hidden, down_proj, preferred_element_type=jnp.float32
    )
    summed_all = lax.psum(partial_value, "tp")
    expert_part = lax.dynamic_slice_in_dim(summed_all, lax.axis_index("tp") * width, width, 0)
    expert_back = expert_part.astype(jnp.bfloat16).reshape(width, experts_here, n_role, CAP)
    back = lax.all_to_all(expert_back, "role", split_axis=2, concat_axis=2, tiled=True)
    back = back.reshape(width, slots).astype(jnp.float32)
    owner = jnp.arange(pairs, dtype=jnp.int32) // topk
    row_hot = (owner[:, None] == jnp.arange(rows_ffn, dtype=jnp.int32)[None, :]).astype(jnp.float32)
    weighted_select = select.astype(jnp.float32) * route_weights.reshape(-1)[:, None]
    combine = jnp.sum(weighted_select[:, :, None] * row_hot[:, None, :], axis=0)
    ffn_out = jnp.einsum("ds,sb->bd", back, combine, precision=lax.Precision.HIGHEST).astype(
        jnp.bfloat16
    )
    return (attention_out, ffn_out)


def solution(mesh):
    return jax.shard_map(
        shards,
        mesh=mesh,
        in_specs=(
            P("role", None),
            P("role", "tp", None),
            P("role"),
            P("role", "tp"),
            P("role", None),
            P("role", None),
            P("role", None, None, "tp"),
            P("role", "tp", None),
        ),
        out_specs=(P("role", "tp"), P("role", "tp")),
        check_vma=False,
    )
```

profile of v0, /device:TPU:32, one launch (start us, length us, event | category | flops | bytes accessed | tf_op | source)
XLA Modules:
  0.0 867.6 jit_solution(3219180449930161840)
XLA Ops:
  9.8 10.2 %all_to_all.10 = bf16[2,4,16,112]{3,2,0,1:T(8,128)(2,1)S(1)} all-to-all(bf16[2,4,16,112]{3,2,0,1:T(8,128)(2,1)S(1)} %copy.54), channel_id=1, replica_groups=mesh['role'=4,'tp'=64] {'role'}, dimensions={1} | all-to-all | bytes 57344 | tf_op jit(solution)/shard_map/all_to_all | solution.py:88
  21.6 1.6 fusion.15
  26.5 117.7 %all-gather = f32[512,64]{1,0:T(8,128)S(1)} all-gather(f32[8,64]{1,0:T(8,128)S(1)} %get-tuple-element.201), channel_id=2, replica_groups=mesh['role'=4,'tp'=64] {'tp'}, dimensions={0}, use_global_device_ids=true | all-gather | bytes 133120 | tf_op jit(solution)/shard_map/all_gather | solution.py:10
  145.0 2.0 fusion.6
  147.1 5.3 fusion.3
  152.4 2.5 convolution_bitcast_fusion
  154.9 503.3 %all-reduce.1 = bf16[7168,2,64]{0,2,1:T(8,128)(2,1)} all-reduce(f32[7168,2,64]{0,2,1:T(8,128)} %convolution_bitcast_fusion), channel_id=1, replica_groups=mesh['role'=4,'tp'=64] {'tp'}, use_global_device_ids=true, to_apply=%region_7.8 | all-reduce | flops 917504 | bytes 5505024 | tf_op jit(solution)/shard_map/psum | solution.py:102
  659.7 5.9 all-to-all-start.1
  665.6 108.1 %all-gather.1 = f32[512,64]{1,0:T(8,128)S(1)} all-gather(f32[8,64]{1,0:T(8,128)S(1)} %fusion.6), channel_id=3, replica_groups=mesh['role'=4,'tp'=64] {'tp'}, dimensions={0}, use_global_device_ids=true | all-gather | bytes 133120 | tf_op jit(solution)/shard_map/all_gather | solution.py:10
  775.5 84.2 %while.19 = (s32[]{:T(128)}, f32[8,64]{1,0:T(8,128)S(1)}, f32[8,64]{1,0:T(8,128)S(1)}, f32[8,64,256]{2,1,0:T(8,128)S(1)}, f32[64,8,64]{2,1,0:T(8,128)S(1)}, /*in...) while((s32[]{:T(128)}, f32[8,64]{1,0:T(8,128)S(1)}, ...), condition=%wide.region_3.4_spmd, body=%wide.region_2.3_spmd.sunk | while | flops 396293 | bytes 1593495 | solution.py:15
  775.5 1.3 fusion.52
  776.9 1.3 fusion.52
  778.2 1.3 fusion.52
  779.5 1.3 fusion.52
  780.9 1.3 fusion.52
  782.2 1.3 fusion.52
  783.5 1.3 fusion.52
  784.9 1.3 fusion.52
  786.2 1.3 fusion.52
  787.6 1.3 fusion.52
  788.9 1.3 fusion.52
  790.2 1.3 fusion.52
  791.6 1.3 fusion.52
  792.9 1.3 fusion.52
  794.2 1.3 fusion.52
  795.6 1.3 fusion.52
  796.9 1.3 fusion.52
  798.2 1.3 fusion.52
  799.6 1.3 fusion.52
  800.9 1.3 fusion.52
  802.2 1.3 fusion.52
  803.6 1.3 fusion.52
  804.9 1.3 fusion.52
  806.3 1.3 fusion.52
  807.6 1.3 fusion.52
  808.9 1.3 fusion.52
  810.3 1.3 fusion.52
  811.6 1.3 fusion.52
  812.9 1.3 fusion.52
  814.3 1.3 fusion.52
  815.6 1.3 fusion.52
  816.9 1.3 fusion.52
  818.3 1.3 fusion.52
  819.6 1.3 fusion.52
  820.9 1.3 fusion.52
  822.3 1.3 fusion.52
  823.6 1.3 fusion.52
  825.0 1.3 fusion.52
  826.3 1.3 fusion.52
  827.6 1.3 fusion.52
  829.0 1.3 fusion.52
  830.3 1.3 fusion.52
  831.6 1.3 fusion.52
  833.0 1.3 fusion.52
  834.3 1.3 fusion.52
  835.6 1.3 fusion.52
  837.0 1.3 fusion.52
  838.3 1.3 fusion.52
  839.6 1.3 fusion.52
  841.0 1.3 fusion.52
  843.7 1.3 fusion.52
  846.3 1.3 fusion.52
  849.0 1.3 fusion.52
  851.7 1.3 fusion.52
  (122 shorter events, 25.3 us)
Async XLA Ops:
  7.2 145.2 %copy-start = (bf16[2,80,7168]{2,1,0:T(8,128)(2,1)S(1)}, bf16[2,80,7168]{2,1,0:T(8,128)(2,1)}, u32[]{:S(2)}) copy-start(bf16[2,80,7168]{2,1,0:T(8,128)(2,1)} %param.17) | copy-start | bytes 6881284
  7.2 16.1 %copy-start.2 = (bf16[8,16384]{1,0:T(8,128)(2,1)S(1)}, bf16[8,16384]{1,0:T(8,128)(2,1)}, u32[]{:S(2)}) copy-start(bf16[8,16384]{1,0:T(8,128)(2,1)} %param.10) | copy-start | bytes 786436
  7.2 139.9 %all-gather.6.cloned.1.call-start = ((), (), s32[]{:S(2)}) async-start(), calls=%async_computation.2 | async-start | bytes 3727360 | tf_op jit(solution)/shard_map/all_gather | solution.py:94
  20.8 753.6 %all-gather.8.cloned.1.call-start = ((), (), s32[]{:S(2)}) async-start(), calls=%async_computation.3 | async-start | bytes 34078720 | tf_op jit(solution)/shard_map/all_gather | solution.py:10
  20.8 2.4 copy-start.3
  23.8 1.3 copy-start.1
  25.1 119.0 %copy-start.4 = (f32[32,3]{0,1:T(4,128)S(1)}, f32[32,3]{0,1:T(4,128)}, u32[]{:S(2)}) copy-start(f32[32,3]{0,1:T(4,128)} %param.15) | copy-start | bytes 1156
  659.7 114.0 %all-to-all-start.1 = ((bf16[112,2,4,16]{0,3,1,2:T(8,128)(2,1)}), bf16[112,2,4,16]{0,3,1,2:T(8,128)(2,1)S(1)}, u32[]{:S(2)}, u32[]{:S(2)}) async-start(bf16[112,2,4,16]{0,3,1,2:T(8,128)(2,1)} %copy.58), calls=%async_computation.1 | async-start | bytes 65536 | tf_op jit(solution)/shard_map/all_to_all | solution.py:105
Sparse Core Ops, SparseCore 0:
  20.9 89.2 all-gather.5
  113.7 258.3 all-gather.7
where the time goes:
time: 872 us; the launch traced here: 868 us
  blocking collectives  739 us (85%)
  other arithmetic  86.8 us (10%)
  between operations  14.2 us (2%)
  matrix products  12.7 us (1%)
    psum x1, blocking collectives, shards(): summed_all = lax.psum(partial_value, 'tp')  503 us
    all_gather x2, blocking collectives, merged(): gathered = jax.tree.map(lambda a: lax.all_gather(a, axis), part)  226 us
    add x63, other arithmetic, join_softmax(): first[2] * scale_first[:, :, None] + second[2] * scale_second[:, :, None]  81.2 us
  transfers between devices with their start and end apart: 3, of which 0 were waited for; matrix products, arithmetic and copies ran while one was open for 2% of the time, Pallas kernels for 0%

commit v1 on v0

v1 whole, which is shorter than its diff:
```python
import jax
import jax.numpy as jnp
from jax import lax
from jax.experimental import pallas as pl
from jax.experimental.pallas import tpu as pltpu
from jax.sharding import Mesh
from jax.sharding import PartitionSpec as P

F32, BF16 = jnp.float32, jnp.bfloat16
VMEM = pl.BlockSpec(memory_space=pltpu.VMEM)
SMEM = pl.BlockSpec(memory_space=pltpu.SMEM)
XY = 16
BLK = 112
ROWS = 128
NX = 2 * BLK
NA = 48


def call(kernel, out_shape, args, specs=None, limit=16 << 20):
    many = isinstance(out_shape, (list, tuple))
    return pl.pallas_call(
        kernel,
        out_shape=out_shape,
        in_specs=specs or [VMEM] * len(args),
        out_specs=[VMEM] * len(out_shape) if many else VMEM,
        compiler_params=pltpu.CompilerParams(vmem_limit_bytes=limit),
    )(*args)


def split3(v):
    hi = v.astype(BF16).astype(F32)
    mid = (v - hi).astype(BF16).astype(F32)
    return hi, mid, (v - hi) - mid


def with_lse(out, lse):
    hi, mid, lo = split3(lse)
    lane = lax.broadcasted_iota(jnp.int32, (out.shape[0], 128), 1)
    tail = jnp.where(lane == 0, hi, jnp.where(lane == 1, mid, jnp.where(lane == 2, lo, 0.0)))
    return jnp.concatenate([out, tail], axis=1)


def lse_of(part):
    return jnp.sum(part[..., 256:], axis=-1, keepdims=True)


def attend_kernel(q_ref, cache_ref, pick_ref, out_ref):
    rows = q_ref.shape[0] * q_ref.shape[1]
    query = q_ref[...].astype(F32).reshape(rows, 256).astype(BF16)
    second = pick_ref[...] == 1
    dims = (((1,), (1,)), ((), ()))
    first_s = lax.dot_general(query, cache_ref[0, :, :256], dims, preferred_element_type=F32)
    second_s = lax.dot_general(query, cache_ref[1, :, :256], dims, preferred_element_type=F32)
    scores = jnp.where(second, second_s, first_s) * (256 ** -0.5)
    top = jnp.max(scores, axis=1, keepdims=True)
    expo = jnp.exp(scores - top)
    total = jnp.sum(expo, axis=1, keepdims=True)
    summed = jnp.dot(
        jnp.where(second, 0.0, expo).astype(BF16), cache_ref[0, :, 256:], preferred_element_type=F32
    ) + jnp.dot(
        jnp.where(second, expo, 0.0).astype(BF16), cache_ref[1, :, 256:], preferred_element_type=F32
    )
    both = with_lse(summed / total, top + jnp.log(total))
    out_ref[...] = both.reshape(out_ref.shape).astype(BF16)


def attend(queries, cache, beam_sequence):
    rows, heads = queries.shape[0], queries.shape[1] // 256
    chunk = 16
    query = queries.reshape(rows, heads, 256).transpose(1, 0, 2)
    pick = jnp.tile(beam_sequence, chunk)[:, None]
    return pl.pallas_call(
        attend_kernel,
        grid=(heads // chunk,),
        out_shape=jax.ShapeDtypeStruct((heads, rows, 384), BF16),
        in_specs=[
            pl.BlockSpec((chunk, rows, 256), lambda i: (i, 0, 0)),
            pl.BlockSpec(cache.shape, lambda i: (0, 0, 0)),
            pl.BlockSpec((chunk * rows, 1), lambda i: (0, 0)),
        ],
        out_specs=pl.BlockSpec((chunk, rows, 384), lambda i: (i, 0, 0)),
        compiler_params=pltpu.CompilerParams(vmem_limit_bytes=20 << 20),
    )(query, cache, pick)


def pair(first, second):
    lse_a, lse_b = lse_of(first), lse_of(second)
    top = jnp.maximum(lse_a, lse_b)
    wa, wb = jnp.exp(lse_a - top), jnp.exp(lse_b - top)
    total = wa + wb
    out = (first[..., :256] * wa + second[..., :256] * wb) / total
    return out, top + jnp.log(total)


def pack_kernel(index_ref, rows_ref, mine_ref, theirs_ref, out_ref, weight_ref):
    out, lse = pair(
        mine_ref[...].astype(F32).reshape(256, 384), theirs_ref[...].astype(F32).reshape(256, 384)
    )
    both = with_lse(out, lse).reshape(2, XY, 8, 384)
    pieces = [both[z, :, :, p * 128 : (p + 1) * 128] for z in range(2) for p in range(3)]
    out_ref[:, NX:, :] = jnp.concatenate(pieces, axis=1).astype(BF16)
    for z in range(2):
        block = jnp.concatenate([rows_ref[2 * r + z] for r in range(4)], axis=0)
        turned = block.astype(F32).T
        if z == 0:
            weight_ref[...] = turned[BLK : BLK + 8] + turned[BLK + 8 :]
        features = turned[:BLK].astype(BF16)
        for p in range(XY):
            out_ref[p, z * BLK : (z + 1) * BLK, :] = features


def ffn_kernel(index_ref, mine_ref, theirs_ref, weight_ref, gate_ref, down_ref, keep_ref, give_ref, x_ref):
    role, core = index_ref[0], index_ref[1]
    for z in range(2):
        for p in range(XY):
            start = (z * XY + p) * 2 * BLK
            x_ref[pl.ds(pl.multiple_of(start + core * BLK, 16), BLK), :] = mine_ref[
                p, z * BLK : (z + 1) * BLK, :
            ]
            x_ref[pl.ds(pl.multiple_of(start + (1 - core) * BLK, 16), BLK), :] = theirs_ref[
                p, z * BLK : (z + 1) * BLK, :
            ]
    units = gate_ref.shape[2]
    both = jnp.dot(
        gate_ref[...].reshape(4 * units, gate_ref.shape[3]), x_ref[...], preferred_element_type=F32
    )
    hidden = []
    for e in range(2):
        gate = both[2 * e * units : (2 * e + 1) * units]
        upper = both[(2 * e + 1) * units : (2 * e + 2) * units]
        weight = weight_ref[pl.ds(2 * role + e, 1), :]
        hidden.append(((gate / (1.0 + jnp.exp(-gate))) * upper * weight).astype(BF16))
    hidden = jnp.concatenate(hidden, axis=0)
    down = down_ref[...].reshape(2 * units, down_ref.shape[2])
    for z in range(2):
        for x in range(4):
            start = (z * 4 + x) * 8 * BLK
            part = lax.dot_general(
                down[:, start : start + 8 * BLK],
                hidden,
                (((0,), (0,)), ((), ())),
                preferred_element_type=F32,
            ).astype(BF16)
            for y in range(4):
                even = part[2 * y * BLK : (2 * y + 1) * BLK]
                odd = part[(2 * y + 1) * BLK : (2 * y + 2) * BLK]
                keep_ref[x * 4 + y, z * BLK : (z + 1) * BLK, :] = jnp.where(core == 0, even, odd)
                give_ref[x * 4 + y, z * BLK : (z + 1) * BLK, :] = jnp.where(core == 0, odd, even)


def add_kernel(a_ref, b_ref, out_ref):
    out_ref[...] = (a_ref[...].astype(F32) + b_ref[...].astype(F32)).astype(BF16)


def sum_kernel(parts_ref, out_ref):
    total = parts_ref[0].astype(F32)
    for p in range(1, XY):
        total += parts_ref[p].astype(F32)
    for z in range(2):
        turned = total[z * BLK : (z + 1) * BLK].T.astype(BF16)
        for r in range(4):
            out_ref[2 * r + z] = turned[32 * r : 32 * (r + 1)]


def last_kernel(parts_ref, out_ref):
    total = parts_ref[0].astype(F32)
    for p in range(1, 8):
        total += parts_ref[p].astype(F32)
    out_ref[...] = total.astype(BF16)


def merge_kernel(index_ref, parts_ref, mine_ref, theirs_ref):
    zhi = index_ref[2]
    parts = parts_ref[:, NX:, :].astype(F32)
    done = []
    for z in range(2):
        pieces = [parts[:, (z * 3 + p) * 8 : (z * 3 + p + 1) * 8, :] for p in range(3)]
        lse = jnp.sum(pieces[2], axis=-1, keepdims=True)
        top = jnp.max(lse, axis=0, keepdims=True)
        weight = jnp.exp(lse - top)
        total = jnp.sum(weight, axis=0)
        out = jnp.concatenate([jnp.sum(p * weight, axis=0) for p in pieces[:2]], axis=1) / total
        done.append(with_lse(out, top[0] + jnp.log(total)))
    mine_ref[...] = jnp.where(zhi == 0, done[0], done[1]).astype(BF16)
    theirs_ref[...] = jnp.where(zhi == 0, done[1], done[0]).astype(BF16)


def finish_kernel(a_ref, b_ref, out_ref):
    out, _ = pair(a_ref[...].astype(F32), b_ref[...].astype(F32))
    out_ref[...] = out.astype(BF16)


def shards(queries, cache, beam_sequence, ffn_input, expert_ids, route_weights, gate_up, down_proj):
    shape = jax.ShapeDtypeStruct
    swap = [(0, 1), (1, 0)]
    role, core, zhi = lax.axis_index("role"), lax.axis_index("core"), lax.axis_index("zhi")
    index = jnp.stack([role, core, zhi]).astype(jnp.int32)

    hits = expert_ids[:, :, None] == jnp.arange(8, dtype=jnp.int32)
    weights = jnp.sum(jnp.where(hits, route_weights[:, :, None], 0.0), axis=1)
    high = lax.reduce_precision(weights, 8, 7)
    low = weights - high
    message = jnp.concatenate([ffn_input, high.astype(BF16), low.astype(BF16)], axis=1)
    rows = lax.all_to_all(
        jnp.broadcast_to(message, (8, 32, 128)), ("role", "zhi"), 0, 0, tiled=True
    )

    attended = attend(queries, cache, beam_sequence).reshape(32, 2, 8, 384)
    mine = lax.dynamic_index_in_dim(attended, core, 1, False)
    theirs = lax.ppermute(lax.dynamic_index_in_dim(attended, 1 - core, 1, False), "core", swap)

    packed, weight = call(
        pack_kernel,
        [shape((XY, NX + NA, 128), BF16), shape((8, 128), F32)],
        (index, rows, mine, theirs),
        [SMEM, VMEM, VMEM, VMEM],
    )
    gathered = lax.all_to_all(packed, ("x", "y"), 0, 0, tiled=True)
    other = lax.ppermute(gathered, "core", swap)

    head, away = call(
        merge_kernel, [shape((8, 384), BF16)] * 2, (index, gathered), [SMEM, VMEM]
    )
    attention_out = call(
        finish_kernel, shape((8, 256), BF16), (head, lax.ppermute(away, "zhi", swap))
    )

    units = gate_up.shape[3]
    keep, give = pl.pallas_call(
        ffn_kernel,
        out_shape=[shape((XY, NX, 128), BF16)] * 2,
        in_specs=[SMEM] + [VMEM] * 5,
        out_specs=[VMEM] * 2,
        scratch_shapes=[pltpu.VMEM((64 * BLK, ROWS), BF16)],
        compiler_params=pltpu.CompilerParams(vmem_limit_bytes=24 << 20),
    )(index, gathered, other, weight, gate_up.transpose(0, 2, 3, 1), down_proj)
    half = call(add_kernel, shape((XY, NX, 128), BF16), (keep, lax.ppermute(give, "core", swap)))
    spread = lax.all_to_all(half, ("x", "y"), 0, 0, tiled=True)
    partial = call(sum_kernel, shape((8, 32, BLK), BF16), (spread,))
    ends = lax.all_to_all(partial, ("role", "zhi"), 0, 0, tiled=True)
    ffn_out = call(last_kernel, shape((32, BLK), BF16), (ends,))
    return (attention_out, ffn_out)


def solution(mesh):
    fine = Mesh(mesh.devices.reshape(4, 2, 4, 4, 2), ("role", "zhi", "x", "y", "core"))
    tp = ("zhi", "x", "y", "core")
    return jax.shard_map(
        shards,
        mesh=fine,
        in_specs=(
            P("role", None),
            P("role", tp, None),
            P("role"),
            P("role", tp),
            P("role", None),
            P("role", None),
            P("role", None, None, tp),
            P("role", tp, None),
        ),
        out_specs=(P("role", tp), P("role", tp)),
        check_vma=False,
    )
```

time: 872 us -> 96.6 us (0.11)
  blocking collectives: 739 us -> 43.1 us
  other arithmetic: 86.8 us -> 0.17 us
  waiting for transfers between devices: 0.06 us -> 14.9 us
  between operations: 14.2 us -> 0.77 us
  Pallas kernels: 0 us -> 13.3 us
  matrix products: 12.7 us -> 0 us
  starting transfers between devices: 5.97 us -> 17.5 us
    psum x1 -> x0, blocking collectives: 503 us -> none  [shards(): summed_all = lax.psum(partial_value, 'tp')]
    all_gather x2 -> x0, blocking collectives: 226 us -> none  [merged(): gathered = jax.tree.map(lambda a: lax.all_gather(a, axis), part)]
    add x126 -> x0, other arithmetic: 82.3 us -> none  [the longest x63 81.2 us: join_softmax(): first[2] * scale_first[:, :, None] + second[2] * scale_second[:, :, None]]
    all_to_all x1 -> x2, blocking collectives: 10.2 us -> 43.1 us  [the longest x1 24.2 us: shards(): gathered = lax.all_to_all(packed, ('x', 'y'), 0, 0, tiled=True)]
    pallas_call x0 -> x8, Pallas kernels: none -> 13.3 us  [the longest x1 5.05 us: shards(): pl.pallas_call(ffn_kernel, out_shape=[shape((XY, NX, 128), BF16)] * 2, in...]
    dot_general x8 -> x0, matrix products: 12.7 us -> none  [the longest x1 5.26 us: shards(): jnp.einsum('erd,edf->erf', lax.all_gather(received, 'tp', axis=2, tiled=T...]
  transfers between devices with their start and end apart: 3 -> 6, of which waited for: 0 -> 4; matrix products, arithmetic and copies ran while one was open for 2% -> 1% of each run, Pallas kernels for 0% -> 1%
where the time goes in v1:
time: 96.6 us; the launch traced here: 96.2 us
  blocking collectives  43.1 us (45%)
  starting transfers between devices  17.5 us (18%)
  waiting for transfers between devices  14.9 us (15%)
  Pallas kernels  13.3 us (14%)
  local copies, waits for them, and re-layouts  6.49 us (7%)
    all_to_all x1, blocking collectives, shards(): gathered = lax.all_to_all(packed, ('x', 'y'), 0, 0, tiled=True)  24.2 us
    all_to_all x1, blocking collectives, shards(): spread = lax.all_to_all(half, ('x', 'y'), 0, 0, tiled=True)  19 us
    all_to_all x1, starting transfers between devices, shards(): lax.all_to_all(jnp.broadcast_to(message, (8, 32, 128)), ('role', 'zhi'),...  8.57 us
    all_to_all x1, waiting for transfers between devices, shards(): lax.all_to_all(jnp.broadcast_to(message, (8, 32, 128)), ('role', 'zhi'),...  6.76 us
    pallas_call x1, Pallas kernels, shards(): pl.pallas_call(ffn_kernel, out_shape=[shape((XY, NX, 128), BF16)] * 2, in...  5.05 us
    unnamed x14, local copies, waits for them, and re-layouts  4.85 us
    ppermute x1, starting transfers between devices, shards(): lax.ppermute(away, 'zhi', swap)  4.56 us
    pallas_call x1, Pallas kernels, attend(): pl.pallas_call(attend_kernel, grid=(heads // chunk,), out_shape=jax.Shape...  4.32 us
  transfers between devices with their start and end apart: 6, of which 4 were waited for; matrix products, arithmetic and copies ran while one was open for 1% of the time, Pallas kernels for 1%

profile of v1, /device:TPU:32, one launch (start us, length us, event | category | flops | bytes accessed | tf_op | source)
XLA Modules:
  0.0 96.2 jit_solution(16593128953484409548)
XLA Ops:
  0.6 0.0 copy-start.6
  0.6 0.0 copy-start.5
  0.7 0.0 copy-start.4
  0.7 0.7 tile.2
  1.3 0.1 broadcast_in_dim_tile.4.pick_ref
  1.4 0.0 copy-start.2
  1.4 1.6 %copy-done.2 = bf16[2,1024,512]{2,1,0:T(8,128)(2,1)S(1)} copy-done((bf16[2,1024,512]{2,1,0:T(8,128)(2,1)S(1)}, bf16[2,1024,512]{2,1,0:T(8,128)(2,1)}, u32[]{:S(2)}) %copy-start.2) | copy-done | bytes 2097176
  3.0 0.0 copy-start.3
  3.0 0.9 copy-done.3
  4.0 4.3 %shard_map.95 = bf16[64,8,384]{2,1,0:T(8,128)(2,1)S(1)} custom-call(bf16[64,8,256]{2,1,0:T(8,128)(2,1)S(1)} %bitcast.18, bf16[2,1024,512]{2,1,0:T(8,128)(2,1)S(1)} %copy-done.2, s32[128,1]{1,0:T(8,128)S(1)} %broadcast_in_dim_tile.4.pick_ref), custom_call_target="tpu_custom_call" | custom-call | tf_op jit(solution)/shard_map/pallas_call | solution.py:72
  8.3 0.0 copy-start.1
  8.3 0.1 dynamic-slice_bitcast_fusion
  8.4 0.1 collective-permute-start
  8.5 0.0 copy-done.6
  8.5 0.0 copy-done.5
  8.5 0.1 copy.20
  8.6 0.1 copy.21
  8.7 0.0 copy-done.4
  8.7 0.1 pad_maximum_fusion
  8.8 0.6 broadcast_in_dim.20
  9.4 8.6 %all-to-all-start = ((bf16[8,32,128]{2,1,0:T(8,128)(2,1)}), bf16[8,32,128]{2,1,0:T(8,128)(2,1)S(1)}, u32[]{:S(2)}, u32[]{:S(2)}) async-start(bf16[8,32,128]{2,1,0:T(8,128)(2,1)} %broadcast_in_dim.20), calls=%async_computation | async-start | bytes 131072 | tf_op jit(solution)/shard_map/all_to_all | solution.py:204
  18.0 0.1 pad_add_fusion.index_ref
  18.1 6.8 %all-to-all-done.rows_ref = bf16[8,32,128]{2,1,0:T(8,128)(2,1)S(1)} async-done(((bf16[8,32,128]{2,1,0:T(8,128)(2,1)}), bf16[8,32,128]{2,1,0:T(8,128)(2,1)S(1)}, u32[]{:S(2)}, u32[]{:S(2)}) %all-to-all-start) | async-done | bytes 65568 | tf_op jit(solution)/shard_map/all_to_all | solution.py:204
  24.8 0.0 collective-permute-done.theirs_ref
  24.8 0.8 shard_map.96
  25.7 24.2 %all_to_all.20.parts_ref.mine_ref = bf16[16,272,128]{2,1,0:T(8,128)(2,1)S(1)} all-to-all(bf16[16,272,128]{2,1,0:T(8,128)(2,1)S(1)} %get-tuple-element.8), channel_id=1, replica_groups=mesh['role'=4,'zhi'=2,'x'=4,'y'=4,'core'=2] {'x','y'}, dimensions={0} | all-to-all | bytes 2228224 | tf_op jit(solution)/shard_map/all_to_all | solution.py:218
  49.9 0.0 collective-permute-start.2
  49.9 2.8 %collective-permute-done.2.theirs_ref = bf16[16,272,128]{2,1,0:T(8,128)(2,1)S(1)} collective-permute-done((bf16[16,272,128]{2,1,0:T(8,128)(2,1)S(1)}, bf16[16,272,128]{2,1,0:T(8,128)(2,1)S(1)}, u32[]{:S(2)}, u32[]{:S(2)}) %collective-permute-start.2) | collective-permute-done | bytes 1114144 | tf_op jit(solution)/shard_map/ppermute | solution.py:219
  52.6 0.0 copy-done.1
  52.6 0.0 copy-start
  52.6 2.3 %copy-done = bf16[2,7168,2,80]{1,3,2,0:T(8,128)(2,1)S(1)} copy-done((bf16[2,7168,2,80]{1,3,2,0:T(8,128)(2,1)S(1)}, bf16[2,7168,2,80]{1,3,2,0:T(8,128)(2,1)}, u32[]{:S(2)}) %copy-start) | copy-done | bytes 4587544
  54.9 5.0 %shard_map.99 = (bf16[16,224,128]{2,1,0:T(8,128)(2,1)S(1)}, bf16[16,224,128]{2,1,0:T(8,128)(2,1)S(1)}) custom-call(s32[3]{0:T(128)S(1)} %pad_add_fusion.index_ref, bf16[16,272,128]{2,1,0:T(8,128)(2,1)S(1)} %all_to_all.20.parts_ref.mine_ref, bf16[16,272,128]{2,1,0:T(8,128)(2,1)S(1)} %collective-permute-done.2.theirs_ref, ...), custom_call_target="tpu_custom_call" | custom-call | tf_op jit(solution)/shard_map/pallas_call | solution.py:229
  60.0 0.2 collective-permute-start.3
  60.2 2.3 %collective-permute-done.3.b_ref = bf16[16,224,128]{2,1,0:T(8,128)(2,1)S(1)} collective-permute-done((bf16[16,224,128]{2,1,0:T(8,128)(2,1)S(1)}, bf16[16,224,128]{2,1,0:T(8,128)(2,1)S(1)}, u32[]{:S(2)}, u32[]{:S(2)}) %collective-permute-start.3) | collective-permute-done | bytes 917536 | tf_op jit(solution)/shard_map/ppermute | solution.py:237
  62.5 0.2 shard_map.100
  62.8 19.0 %all_to_all.21.parts_ref = bf16[16,224,128]{2,1,0:T(8,128)(2,1)S(1)} all-to-all(bf16[16,224,128]{2,1,0:T(8,128)(2,1)S(1)} %shard_map.100), channel_id=1, replica_groups=mesh['role'=4,'zhi'=2,'x'=4,'y'=4,'core'=2] {'x','y'}, dimensions={0} | all-to-all | bytes 1835008 | tf_op jit(solution)/shard_map/all_to_all | solution.py:238
  81.7 0.8 shard_map.101
  82.5 4.0 %all-to-all-start.3 = ((bf16[8,32,112]{2,1,0:T(8,128)(2,1)}), bf16[8,32,112]{2,1,0:T(8,128)(2,1)S(1)}, u32[]{:S(2)}, u32[]{:S(2)}) async-start(bf16[8,32,112]{2,1,0:T(8,128)(2,1)} %shard_map.101), calls=%async_computation.3 | async-start | bytes 131072 | tf_op jit(solution)/shard_map/all_to_all | solution.py:240
  86.6 0.7 shard_map.97
  87.3 4.6 %collective-permute-start.1 = (bf16[8,384]{1,0:T(8,128)(2,1)S(1)}, bf16[8,384]{1,0:T(8,128)(2,1)S(1)}, u32[]{:S(2)}, u32[]{:S(2)}) collective-permute-start(bf16[8,384]{1,0:T(8,128)(2,1)S(1)} %get-tuple-element.10), channel_id=1, source_target_pairs={{0,32},{32,0},{1,33},{33,1},{2,34},{34,2},{3,35},{35,3},{4,36},{36... | collective-permute-start | bytes 18440 | tf_op jit(solution)/shard_map/ppermute | solution.py:225
  91.8 3.1 %collective-permute-done.1.b_ref = bf16[8,384]{1,0:T(8,128)(2,1)S(1)} collective-permute-done((bf16[8,384]{1,0:T(8,128)(2,1)S(1)}, bf16[8,384]{1,0:T(8,128)(2,1)S(1)}, u32[]{:S(2)}, u32[]{:S(2)}) %collective-permute-start.1) | collective-permute-done | bytes 6176 | tf_op jit(solution)/shard_map/ppermute | solution.py:225
  94.9 0.7 shard_map.98
  95.6 0.0 all-to-all-done.3.parts_ref
  95.6 0.6 shard_map.102
  (2 shorter events, 0.0 us)
Async XLA Ops:
  0.6 7.8 %copy-start.6 = (s32[32,3]{0,1:T(4,128)S(1)}, s32[32,3]{0,1:T(4,128)}, u32[]{:S(2)}) copy-start(s32[32,3]{0,1:T(4,128)} %param.12) | copy-start | bytes 1156
  0.6 7.8 %copy-start.5 = (f32[32,3]{0,1:T(4,128)S(1)}, f32[32,3]{0,1:T(4,128)}, u32[]{:S(2)}) copy-start(f32[32,3]{0,1:T(4,128)} %param.13) | copy-start | bytes 1156
  0.7 8.1 %copy-start.4 = (bf16[32,112]{1,0:T(8,128)(2,1)S(1)}, bf16[32,112]{1,0:T(8,128)(2,1)}, u32[]{:S(2)}) copy-start(bf16[32,112]{1,0:T(8,128)(2,1)} %param.11) | copy-start | bytes 21508
  1.4 1.6 %copy-start.2 = (bf16[2,1024,512]{2,1,0:T(8,128)(2,1)S(1)}, bf16[2,1024,512]{2,1,0:T(8,128)(2,1)}, u32[]{:S(2)}) copy-start(bf16[2,1024,512]{2,1,0:T(8,128)(2,1)} %cache_ref.1) | copy-start | bytes 6291460
  3.0 0.9 copy-start.3
  8.3 44.3 %copy-start.1 = (bf16[2,80,7168]{2,1,0:T(8,128)(2,1)S(1)}, bf16[2,80,7168]{2,1,0:T(8,128)(2,1)}, u32[]{:S(2)}) copy-start(bf16[2,80,7168]{2,1,0:T(8,128)(2,1)} %down_ref.1) | copy-start | bytes 6881284
  8.4 16.5 %collective-permute-start = (bf16[32,8,384]{2,1,0:T(8,128)(2,1)S(1)}, bf16[32,8,384]{2,1,0:T(8,128)(2,1)S(1)}, u32[]{:S(2)}, u32[]{:S(2)}) collective-permute-start(bf16[32,8,384]{2,1,0:T(8,128)(2,1)S(1)} %get-tuple-element.14), channel_id=1, source_target_pairs={{0,1},{1,0},{2,3},{3,2},{4,5},{5,4},{6,7},{7,6},{8,9},{9,8},{10,11... | collective-permute-start | bytes 589832 | tf_op jit(solution)/shard_map/ppermute | solution.py:210
  9.4 15.4 %all-to-all-start = ((bf16[8,32,128]{2,1,0:T(8,128)(2,1)}), bf16[8,32,128]{2,1,0:T(8,128)(2,1)S(1)}, u32[]{:S(2)}, u32[]{:S(2)}) async-start(bf16[8,32,128]{2,1,0:T(8,128)(2,1)} %broadcast_in_dim.20), calls=%async_computation | async-start | bytes 131072 | tf_op jit(solution)/shard_map/all_to_all | solution.py:204
  49.9 2.8 %collective-permute-start.2 = (bf16[16,272,128]{2,1,0:T(8,128)(2,1)S(1)}, bf16[16,272,128]{2,1,0:T(8,128)(2,1)S(1)}, u32[]{:S(2)}, u32[]{:S(2)}) collective-permute-start(bf16[16,272,128]{2,1,0:T(8,128)(2,1)S(1)} %all_to_all.20.parts_ref.mine_ref), channel_id=1, source_target_pairs={{0,1},{1,0},{2,3},{3,2},{4,5},{5,4},{6,7},{7,6},{8,9},{9,8},{10,11... | collective-permute-start | bytes 3342344 | tf_op jit(solution)/shard_map/ppermute | solution.py:219
  52.6 2.3 %copy-start = (bf16[2,7168,2,80]{1,3,2,0:T(8,128)(2,1)S(1)}, bf16[2,7168,2,80]{1,3,2,0:T(8,128)(2,1)}, u32[]{:S(2)}) copy-start(bf16[2,7168,2,80]{1,3,2,0:T(8,128)(2,1)} %param.14) | copy-start | bytes 13762564
  60.0 2.6 %collective-permute-start.3 = (bf16[16,224,128]{2,1,0:T(8,128)(2,1)S(1)}, bf16[16,224,128]{2,1,0:T(8,128)(2,1)S(1)}, u32[]{:S(2)}, u32[]{:S(2)}) collective-permute-start(bf16[16,224,128]{2,1,0:T(8,128)(2,1)S(1)} %get-tuple-element.13), channel_id=1, source_target_pairs={{0,1},{1,0},{2,3},{3,2},{4,5},{5,4},{6,7},{7,6},{8,9},{9,8},{10,11... | collective-permute-start | bytes 2752520 | tf_op jit(solution)/shard_map/ppermute | solution.py:237
  82.5 13.0 %all-to-all-start.3 = ((bf16[8,32,112]{2,1,0:T(8,128)(2,1)}), bf16[8,32,112]{2,1,0:T(8,128)(2,1)S(1)}, u32[]{:S(2)}, u32[]{:S(2)}) async-start(bf16[8,32,112]{2,1,0:T(8,128)(2,1)} %shard_map.101), calls=%async_computation.3 | async-start | bytes 131072 | tf_op jit(solution)/shard_map/all_to_all | solution.py:240
  87.3 7.6 %collective-permute-start.1 = (bf16[8,384]{1,0:T(8,128)(2,1)S(1)}, bf16[8,384]{1,0:T(8,128)(2,1)S(1)}, u32[]{:S(2)}, u32[]{:S(2)}) collective-permute-start(bf16[8,384]{1,0:T(8,128)(2,1)S(1)} %get-tuple-element.10), channel_id=1, source_target_pairs={{0,32},{32,0},{1,33},{33,1},{2,34},{34,2},{3,35},{35,3},{4,36},{36... | collective-permute-start | bytes 18440 | tf_op jit(solution)/shard_map/ppermute | solution.py:225

commit v2 on v1

v2 whole, which is shorter than its diff:
```python
import jax
import jax.numpy as jnp
from jax import lax
from jax.experimental import pallas as pl
from jax.experimental.pallas import tpu as pltpu
from jax.sharding import Mesh
from jax.sharding import PartitionSpec as P

F32, BF16 = jnp.float32, jnp.bfloat16
VMEM = pl.BlockSpec(memory_space=pltpu.VMEM)
SMEM = pl.BlockSpec(memory_space=pltpu.SMEM)
ANY = pl.BlockSpec(memory_space=pl.ANY)
HBM = pl.BlockSpec(memory_space=pltpu.HBM)
FULL = 62 << 20
XY = 16
BLK = 112
ROWS = 128
NX = 2 * BLK
NA = 48


def call(kernel, out_shape, args, specs=None, limit=16 << 20, scratch=(), cost=None, outs=None):
    many = isinstance(out_shape, (list, tuple))
    return pl.pallas_call(
        kernel,
        out_shape=out_shape,
        in_specs=specs or [VMEM] * len(args),
        out_specs=outs or ([VMEM] * len(out_shape) if many else VMEM),
        scratch_shapes=scratch,
        cost_estimate=cost,
        compiler_params=pltpu.CompilerParams(vmem_limit_bytes=limit),
    )(*args)


def split3(v):
    hi = v.astype(BF16).astype(F32)
    mid = (v - hi).astype(BF16).astype(F32)
    return hi, mid, (v - hi) - mid


def with_lse(out, lse):
    hi, mid, lo = split3(lse)
    lane = lax.broadcasted_iota(jnp.int32, (out.shape[0], 128), 1)
    tail = jnp.where(lane == 0, hi, jnp.where(lane == 1, mid, jnp.where(lane == 2, lo, 0.0)))
    return jnp.concatenate([out, tail], axis=1)


def lse_of(part):
    return jnp.sum(part[..., 256:], axis=-1, keepdims=True)


def prep_kernel(x_hbm, ids_hbm, route_hbm, out_ref, rows_ref, ids_ref, route_ref, turn_ref, sems):
    copies = [
        pltpu.make_async_copy(src, dst, sems.at[i])
        for i, (src, dst) in enumerate(((ids_hbm, ids_ref), (route_hbm, route_ref), (x_hbm, rows_ref)))
    ]
    for copy in copies:
        copy.start()
    turn_ref[...] = jnp.zeros_like(turn_ref)
    expert = lax.broadcasted_iota(jnp.int32, (8, 32), 0)
    weight = jnp.zeros((8, 32), F32)
    copies[0].wait()
    copies[1].wait()
    for k in range(3):
        weight += jnp.where(ids_ref[k : k + 1, :] == expert, route_ref[k : k + 1, :], 0.0)
    high = weight.astype(BF16).astype(F32)
    turn_ref[BLK : BLK + 8, :32] = high
    turn_ref[BLK + 8 :, :32] = weight - high
    turned = turn_ref[...].T[:32]
    copies[2].wait()
    wide = jnp.concatenate([rows_ref[...].astype(F32), jnp.zeros((32, 128 - BLK), F32)], axis=1)
    message = (wide + turned).astype(BF16)
    for p in range(8):
        out_ref[p] = message


def pack_kernel(rows_ref, out_ref, weight_ref):
    for z in range(2):
        block = jnp.concatenate([rows_ref[2 * r + z] for r in range(4)], axis=0)
        turned = block.astype(F32).T
        if z == 0:
            weight_ref[...] = turned[BLK : BLK + 8] + turned[BLK + 8 :]
        features = turned[:BLK].astype(BF16)
        for p in range(XY):
            out_ref[p, z * BLK : (z + 1) * BLK, :] = features


def attend(seq_ref, queries, caches, waits, out_ref):
    steps = len(queries)
    rows = queries[0].shape[0]
    place = lax.broadcasted_iota(jnp.int32, (rows, 1), 0) % 8
    pick = jnp.zeros((rows, 1), jnp.int32)
    for r in range(8):
        pick = jnp.where(place == r, seq_ref[r], pick)
    second = pick == 1
    dims = (((1,), (1,)), ((), ()))
    scores = [[] for _ in range(steps)]
    for k in range(2):
        waits[k]()
        for step in range(steps):
            both = [
                lax.dot_general(
                    queries[step], caches[k, s, :, :256], dims, preferred_element_type=F32
                )
                for s in range(2)
            ]
            scores[step].append(jnp.where(second, both[1], both[0]) * (256 ** -0.5))
    for step in range(steps):
        top = jnp.maximum(*(jnp.max(v, axis=1, keepdims=True) for v in scores[step]))
        total, summed = 0.0, 0.0
        for k in range(2):
            expo = jnp.exp(scores[step][k] - top)
            total += jnp.sum(expo, axis=1, keepdims=True)
            for s in range(2):
                part = jnp.where(second == (s == 1), expo, 0.0).astype(BF16)
                summed += jnp.dot(part, caches[k, s, :, 256:], preferred_element_type=F32)
        both = with_lse(summed / total, top + jnp.log(total)).reshape(rows // 8, 8, 384)
        out_ref[step * (rows // 8) : (step + 1) * (rows // 8)] = both.astype(BF16)


def local_kernel(
    seq_ref, q_hbm, mine_hbm, theirs_hbm, gate_hbm, got_gate_hbm, down_hbm, got_down_hbm, after_ref,
    attended_ref, out_g0_hbm, out_g1_hbm, out_d_ref,
    q_ref, cache_ref, in_ref, out_g_ref, cache_sems, in_sems, out_sems,
):
    core = lax.axis_index("core")
    units = in_ref.shape[1]
    positions = cache_ref.shape[2] // 4
    q_load = pltpu.make_async_copy(q_hbm.at[:, core], q_ref, cache_sems.at[16])
    q_load.start()
    cache_loads = []
    for k, ref in enumerate((mine_hbm, theirs_hbm)):
        for s in range(2):
            for i in range(4):
                at = (s, pl.ds(i * positions, positions))
                cache_loads.append(
                    pltpu.make_async_copy(
                        ref.at[at], cache_ref.at[(k,) + at], cache_sems.at[len(cache_loads)]
                    )
                )
                cache_loads[-1].start(priority=i % 2)
    sources = [ref.at[e, g] for ref in (gate_hbm, got_gate_hbm) for e in range(2) for g in range(2)]
    sources += [ref.at[e] for ref in (down_hbm, got_down_hbm) for e in range(2)]
    loads = [
        pltpu.make_async_copy(source, in_ref.at[i], in_sems.at[i]) for i, source in enumerate(sources)
    ]
    for i, load in enumerate(loads):
        load.start(priority=i % 2)

    def wait(k):
        for load in cache_loads[8 * k : 8 * k + 8]:
            load.wait()

    q_load.wait()
    queries = [
        q_ref[step * 16 : (step + 1) * 16].astype(F32).reshape(128, 256).astype(BF16)
        for step in range(2)
    ]
    attend(seq_ref, queries, cache_ref, [lambda: wait(0), lambda: wait(1)], attended_ref)

    stores = []
    for i in range(8):
        for piece in range(4):
            at = (piece, i // 4, pl.ds((i % 4) * units, units))
            to = (out_g0_hbm, out_g1_hbm)[piece // 2].at[(piece % 2,) + at[1:]]
            stores.append(
                pltpu.make_async_copy(out_g_ref.at[at], to, out_sems.at[len(stores)])
            )
    for i, load in enumerate(loads):
        load.wait()
        out = out_g_ref if i < 8 else out_d_ref
        k, row = (i // 4, (i % 4) * units) if i < 8 else ((i - 8) // 2, (i % 2) * units)
        for parity in range(2):

            @pl.when(core == parity)
            def _():
                for piece in range(4):
                    wide = [
                        in_ref[i, :, (z * 4 + piece) * 8 * BLK : (z * 4 + piece + 1) * 8 * BLK]
                        for z in range(2)
                    ]
                    parts = [
                        wide[z][:, (2 * p + parity) * BLK : (2 * p + parity + 1) * BLK]
                        for p in range(4)
                        for z in range(2)
                    ]
                    out[piece, k, row : row + units, :] = jnp.concatenate(parts, axis=1)

        for store in stores[4 * i : 4 * i + 4] if i < 8 else []:
            store.start()
    for store in stores:
        store.wait()


def up_first_kernel(rows_ref, gate_ref, out_ref):
    total = 0.0
    for piece in range(2):
        rows = rows_ref[4 * piece : 4 * piece + 4].reshape(8 * BLK, ROWS)
        total += jnp.dot(
            gate_ref[piece].reshape(-1, 8 * BLK), rows, preferred_element_type=F32
        )
    out_ref[...] = total.reshape(out_ref.shape)


def up_second_kernel(rows_ref, gate_ref, before_ref, out_ref):
    total = before_ref[...].reshape(-1, ROWS)
    for piece in range(2):
        rows = rows_ref[8 + 4 * piece : 12 + 4 * piece].reshape(8 * BLK, ROWS)
        total += jnp.dot(
            gate_ref[piece].reshape(-1, 8 * BLK), rows, preferred_element_type=F32
        )
    out_ref[...] = total.reshape(out_ref.shape)


def activate(both, weight_ref, role, units):
    hidden = []
    for e in range(2):
        gate = both[2 * e * units : (2 * e + 1) * units]
        upper = both[(2 * e + 1) * units : (2 * e + 2) * units]
        weight = weight_ref[pl.ds(2 * role + e, 1), :]
        hidden.append(((gate / (1.0 + jnp.exp(-gate))) * upper * weight).astype(BF16))
    return jnp.concatenate(hidden, axis=0)


def down_kernel(mine_ref, theirs_ref, weight_ref, down_ref, attended_ref, out_ref):
    role = lax.axis_index("role")
    units = mine_ref.shape[1] // 4
    hidden = [
        activate(mine_ref[k] + theirs_ref[1 - k], weight_ref, role, units) for k in range(2)
    ]
    dims = (((0,), (0,)), ((), ()))
    for piece in range(4):
        part = (
            lax.dot_general(down_ref[piece, 0], hidden[0], dims, preferred_element_type=F32)
            + lax.dot_general(down_ref[piece, 1], hidden[1], dims, preferred_element_type=F32)
        ).astype(BF16)
        out_ref[4 * piece : 4 * piece + 4, :NX, :] = part.reshape(4, NX, ROWS)
    both = attended_ref[...].astype(F32).reshape(2, XY, 8, 384)
    pieces = [both[z, :, :, p * 128 : (p + 1) * 128] for z in range(2) for p in range(3)]
    out_ref[:, NX:, :] = jnp.concatenate(pieces, axis=1).astype(BF16)


def turn_kernel(parts_ref, out_ref):
    total = parts_ref[0, :NX].astype(F32)
    for p in range(1, XY):
        total += parts_ref[p, :NX].astype(F32)
    parts = parts_ref[:, NX:, :].astype(F32)
    for z in range(2):
        pieces = [parts[:, (z * 3 + p) * 8 : (z * 3 + p + 1) * 8, :] for p in range(3)]
        lse = jnp.sum(pieces[2], axis=-1, keepdims=True)
        top = jnp.max(lse, axis=0, keepdims=True)
        weight = jnp.exp(lse - top)
        norm = jnp.sum(weight, axis=0)
        out = jnp.concatenate([jnp.sum(p * weight, axis=0) for p in pieces[:2]], axis=1) / norm
        head = with_lse(out, top[0] + jnp.log(norm))
        tail = [head[:, p * 128 : (p + 1) * 128] for p in range(3)] + [jnp.zeros((8, 128), F32)]
        tail = jnp.concatenate(tail, axis=0)
        turned = jnp.concatenate(
            [total[z * BLK : (z + 1) * BLK].T, jnp.zeros((ROWS, 128 - BLK), F32)], axis=1
        )
        for r in range(4):
            both = jnp.concatenate([turned[32 * r : 32 * (r + 1)], tail], axis=0)
            out_ref[2 * r + z] = both.astype(BF16)


def last_kernel(parts_ref, attention_ref, ffn_ref):
    total = parts_ref[0, :32].astype(F32)
    for p in range(1, 8):
        total += parts_ref[p, :32].astype(F32)
    ffn_ref[...] = total[:, :BLK].astype(BF16)
    role = lax.axis_index("role")
    heads = [parts_ref[2 * role + z, 32:].astype(F32) for z in range(2)]
    lse = [jnp.sum(h[16:24], axis=-1, keepdims=True) for h in heads]
    top = jnp.maximum(lse[0], lse[1])
    weight = [jnp.exp(v - top) for v in lse]
    out = [
        (heads[0][half] * weight[0] + heads[1][half] * weight[1]) / (weight[0] + weight[1])
        for half in (slice(0, 8), slice(8, 16))
    ]
    attention_ref[...] = jnp.concatenate(out, axis=1).astype(BF16)


def shards(queries, cache, beam_sequence, ffn_input, expert_ids, route_weights, gate_up, down_proj):
    shape = jax.ShapeDtypeStruct
    swap = [(0, 1), (1, 0)]

    message = call(
        prep_kernel,
        shape((8, 32, 128), BF16),
        (ffn_input, expert_ids.T, route_weights.T),
        [HBM] * 3,
        FULL,
        scratch=[
            pltpu.VMEM((32, BLK), BF16),
            pltpu.VMEM((3, 32), jnp.int32),
            pltpu.VMEM((3, 32), F32),
            pltpu.VMEM((128, 128), F32),
            pltpu.SemaphoreType.DMA((3,)),
        ],
    )
    rows = lax.all_to_all(message, ("role", "zhi"), 0, 0, tiled=True)
    packed, weight = call(pack_kernel, [shape((XY, NX, 128), BF16), shape((8, 128), F32)], (rows,))
    gathered = lax.all_to_all(packed, ("x", "y"), 0, 0, tiled=True)

    query = queries.reshape(8, 32, 2, 256).transpose(1, 2, 0, 3)
    gate = gate_up.transpose(0, 2, 3, 1)
    units = gate_up.shape[3]
    pairs = [w for a in (cache, gate, down_proj) for w in (a, lax.ppermute(a, "core", swap))]
    attended, gate_0, gate_1, down_c = call(
        local_kernel,
        [
            shape((32, 8, 384), BF16),
            shape((2, 2, 4 * units, 8 * BLK), BF16),
            shape((2, 2, 4 * units, 8 * BLK), BF16),
            shape((4, 2, 2 * units, 8 * BLK), BF16),
        ],
        (beam_sequence, query, *pairs, packed),
        [SMEM] + [HBM] * 7 + [ANY],
        FULL,
        [
            pltpu.VMEM((32, 8, 256), BF16),
            pltpu.VMEM((2,) + cache.shape, BF16),
            pltpu.VMEM((12, units, 64 * BLK), BF16),
            pltpu.VMEM((4, 2, 4 * units, 8 * BLK), BF16),
            pltpu.SemaphoreType.DMA((17,)),
            pltpu.SemaphoreType.DMA((12,)),
            pltpu.SemaphoreType.DMA((32,)),
        ],
        pl.CostEstimate(flops=1 << 31, bytes_accessed=24 << 20, transcendentals=1 << 19),
        [VMEM, HBM, HBM, VMEM],
    )

    first = shape((2, 4 * units, ROWS), F32)
    first = call(up_first_kernel, first, (gathered, gate_0))
    first = call(up_second_kernel, first, (gathered, gate_1, first))
    half = call(
        down_kernel,
        shape((XY, NX + NA, 128), BF16),
        (first, lax.ppermute(first, "core", swap), weight, down_c, attended),
    )
    spread = lax.all_to_all(half, ("x", "y"), 0, 0, tiled=True)
    partial = call(turn_kernel, shape((8, 64, 128), BF16), (spread,))
    ends = lax.all_to_all(partial, ("role", "zhi"), 0, 0, tiled=True)
    attention_out, ffn_out = call(
        last_kernel, [shape((8, 256), BF16), shape((32, BLK), BF16)], (ends,)
    )
    return (attention_out, ffn_out)


def solution(mesh):
    fine = Mesh(mesh.devices.reshape(4, 2, 4, 4, 2), ("role", "zhi", "x", "y", "core"))
    tp = ("zhi", "x", "y", "core")
    return jax.shard_map(
        shards,
        mesh=fine,
        in_specs=(
            P("role", None),
            P("role", tp, None),
            P("role"),
            P("role", tp),
            P("role", None),
            P("role", None),
            P("role", None, None, tp),
            P("role", tp, None),
        ),
        out_specs=(P("role", tp), P("role", tp)),
        check_vma=False,
    )
```

time: 96.6 us -> 83.7 us (0.87)
  waiting for transfers between devices: 14.9 us -> 3.59 us
  starting transfers between devices: 17.5 us -> 7.82 us
  blocking collectives: 43.1 us -> 49.3 us
  Pallas kernels: 13.3 us -> 19.2 us
  local copies, waits for them, and re-layouts: 6.49 us -> 2.53 us
    pallas_call x6 -> x8, Pallas kernels: 3.89 us -> 19.2 us  [call(): pl.pallas_call(kernel, out_shape=out_shape, in_specs=specs or [VMEM] * le...]
    pallas_call x2 -> x0, Pallas kernels: 9.37 us -> none  [the longest x1 5.05 us: shards(): pl.pallas_call(ffn_kernel, out_shape=[shape((XY, NX, 128), BF16)] * 2, in...]
    ppermute x4, waiting for transfers between devices: 8.15 us -> 1.62 us  [the longest x1 1.62 us: shards(): lax.ppermute(first, 'core', swap)]
    all_to_all x2 -> x1, starting transfers between devices: 12.6 us -> 7.03 us  [shards(): gathered = lax.all_to_all(packed, ('x', 'y'), 0, 0, tiled=True)]
    all_to_all x2 -> x1, waiting for transfers between devices: 6.76 us -> 1.97 us  [shards(): gathered = lax.all_to_all(packed, ('x', 'y'), 0, 0, tiled=True)]
    all_to_all x1, blocking collectives: 19 us -> 23.2 us  [shards(): spread = lax.all_to_all(half, ('x', 'y'), 0, 0, tiled=True)]
    ppermute x4, starting transfers between devices: 4.88 us -> 0.79 us  [the longest x3 0.69 us: shards(): lax.ppermute(a, 'core', swap)]
    unnamed x14 -> x8, local copies, waits for them, and re-layouts: 4.85 us -> 2.53 us
  transfers between devices with their start and end apart: 6 -> 5, of which waited for: 4 -> 2; matrix products, arithmetic and copies ran while one was open for 1% -> 0% of each run, Pallas kernels for 1% -> 19%
where the time goes in v2:
time: 83.7 us; the launch traced here: 83.3 us
  blocking collectives  49.3 us (59%)
  Pallas kernels  19.2 us (23%)
  starting transfers between devices  7.82 us (9%)
  waiting for transfers between devices  3.59 us (4%)
  local copies, waits for them, and re-layouts  2.53 us (3%)
    all_to_all x1, blocking collectives, shards(): spread = lax.all_to_all(half, ('x', 'y'), 0, 0, tiled=True)  23.2 us
    pallas_call x8, Pallas kernels, call(): pl.pallas_call(kernel, out_shape=out_shape, in_specs=specs or [VMEM] * le...  19.2 us
    all_to_all x1, blocking collectives, shards(): rows = lax.all_to_all(message, ('role', 'zhi'), 0, 0, tiled=True)  15.4 us
    all_to_all x1, blocking collectives, shards(): ends = lax.all_to_all(partial, ('role', 'zhi'), 0, 0, tiled=True)  10.7 us
    all_to_all x1, starting transfers between devices, shards(): gathered = lax.all_to_all(packed, ('x', 'y'), 0, 0, tiled=True)  7.03 us
    unnamed x8, local copies, waits for them, and re-layouts  2.53 us
    all_to_all x1, waiting for transfers between devices, shards(): gathered = lax.all_to_all(packed, ('x', 'y'), 0, 0, tiled=True)  1.97 us
  transfers between devices with their start and end apart: 5, of which 2 were waited for; matrix products, arithmetic and copies ran while one was open for 0% of the time, Pallas kernels for 19%

profile of v2, /device:TPU:32, one launch (start us, length us, event | category | flops | bytes accessed | tf_op | source)
XLA Modules:
  0.0 83.3 jit_solution(3458743859086123183)
XLA Ops:
  0.6 0.1 collective-permute-start.1
  0.7 0.5 collective-permute-start.2
  1.2 0.1 collective-permute-start
  1.3 1.4 %shard_map.95 = bf16[8,32,128]{2,1,0:T(8,128)(2,1)} custom-call(bf16[32,112]{1,0:T(8,128)(2,1)} %x_hbm.1, s32[3,32]{1,0:T(4,128)} %bitcast.9, f32[3,32]{1,0:T(4,128)} %bitcast.10), custom_call_target="tpu_custom_call" | custom-call | tf_op jit(solution)/shard_map/pallas_call | solution.py:24
  2.8 15.4 %all_to_all.20.rows_ref = bf16[8,32,128]{2,1,0:T(8,128)(2,1)S(1)} all-to-all(bf16[8,32,128]{2,1,0:T(8,128)(2,1)} %shard_map.95), channel_id=1, replica_groups=mesh['role'=4,'zhi'=2,'x'=4,'y'=4,'core'=2] {'role','zhi'}, dimensions={0} | all-to-all | bytes 131072 | tf_op jit(solution)/shard_map/all_to_all | solution.py:301
  18.2 1.1 %shard_map.96 = (bf16[16,224,128]{2,1,0:T(8,128)(2,1)}, f32[8,128]{1,0:T(8,128)S(1)}) custom-call(bf16[8,32,128]{2,1,0:T(8,128)(2,1)S(1)} %all_to_all.20.rows_ref), custom_call_target="tpu_custom_call" | custom-call | tf_op jit(solution)/shard_map/pallas_call | solution.py:24
  19.2 7.0 %all-to-all-start.1 = ((bf16[16,224,128]{2,1,0:T(8,128)(2,1)}), bf16[16,224,128]{2,1,0:T(8,128)(2,1)S(1)}, u32[]{:S(2)}, u32[]{:S(2)}) async-start(bf16[16,224,128]{2,1,0:T(8,128)(2,1)} %get-tuple-element.8.after_ref), calls=%async_computation.1 | async-start | bytes 1835008 | tf_op jit(solution)/shard_map/all_to_all | solution.py:303
  26.3 0.0 collective-permute-done.theirs_hbm
  26.3 0.0 collective-permute-done.2.got_down_hbm
  26.3 0.0 collective-permute-done.1.got_gate_hbm
  26.3 13.2 %shard_map.97 = (bf16[32,8,384]{2,1,0:T(8,128)(2,1)}, bf16[2,2,320,896]{3,2,1,0:T(8,128)(2,1)}, bf16[2,2,320,896]{3,2,1,0:T(8,128)(2,1)}, bf16[4,2,160,896]{3,2,1,0:T(8,128)(2,1)}) custom-call(s32[8]{0:T(128)} %seq_ref.1, bf16[32,2,8,256]{3,2,1,0:T(8,128)(2,1)} %bitcast.8, bf16[2,1024,512]{2,1,0:T(8,128)(2,1)} %mine_hbm.1, ...), custom_call_target="tpu_custom_call" | custom-call | flops 2147483648 | bytes 25165824 | tf_op jit(solution)/shard_map/pallas_call | solution.py:24
  39.5 2.0 %all-to-all-done.1.rows_ref = bf16[16,224,128]{2,1,0:T(8,128)(2,1)S(1)} async-done(((bf16[16,224,128]{2,1,0:T(8,128)(2,1)}), bf16[16,224,128]{2,1,0:T(8,128)(2,1)S(1)}, u32[]{:S(2)}, u32[]{:S(2)}) %all-to-all-start.1) | async-done | bytes 917536 | tf_op jit(solution)/shard_map/all_to_all | solution.py:303
  41.4 0.0 copy-start.1
  41.4 1.6 %copy-done.1 = bf16[2,2,320,896]{3,2,1,0:T(8,128)(2,1)S(1)} copy-done((bf16[2,2,320,896]{3,2,1,0:T(8,128)(2,1)S(1)}, bf16[2,2,320,896]{3,2,1,0:T(8,128)(2,1)}, u32[]{:S(2)}) %copy-start.1) | copy-done | bytes 2293784
  43.1 0.0 copy-start.2
  43.1 0.7 shard_map.98.before_ref
  43.8 0.0 copy-start
  43.8 0.0 copy-start.3
  43.9 0.9 %copy-done.2 = bf16[2,2,320,896]{3,2,1,0:T(8,128)(2,1)S(1)} copy-done((bf16[2,2,320,896]{3,2,1,0:T(8,128)(2,1)S(1)}, bf16[2,2,320,896]{3,2,1,0:T(8,128)(2,1)}, u32[]{:S(2)}) %copy-start.2) | copy-done | bytes 2293784
  44.7 0.7 shard_map.99.mine_ref
  45.5 0.1 collective-permute-start.3
  45.6 1.6 %collective-permute-done.3.theirs_ref = f32[2,320,128]{2,1,0:T(8,128)S(1)} collective-permute-done((f32[2,320,128]{2,1,0:T(8,128)S(1)}, f32[2,320,128]{2,1,0:T(8,128)S(1)}, u32[]{:S(2)}, u32[]{:S(2)}) %collective-permute-start.3) | collective-permute-done | bytes 327712 | tf_op jit(solution)/shard_map/ppermute | solution.py:339
  47.2 0.0 copy-done
  47.2 0.0 copy-done.3
  47.2 1.2 %shard_map.100 = bf16[16,272,128]{2,1,0:T(8,128)(2,1)S(1)} custom-call(f32[2,320,128]{2,1,0:T(8,128)S(1)} %shard_map.99.mine_ref, f32[2,320,128]{2,1,0:T(8,128)S(1)} %collective-permute-done.3.theirs_ref, f32[8,128]{1,0:T(8,128)S(1)} %get-tuple-element.11.weight_ref, bf16[4,2,160,896]{3,2,1,0:T(8,128)(2,1)S(1)} %copy-done, bf16[32,8,384]{2,1,0:T(8,128)(2,1)S(1)} %copy-done.3), custom_call_target="tpu_custom_call" | custom-call | tf_op jit(solution)/shard_map/pallas_call | solution.py:24
  48.4 23.2 %all_to_all.21.parts_ref = bf16[16,272,128]{2,1,0:T(8,128)(2,1)S(1)} all-to-all(bf16[16,272,128]{2,1,0:T(8,128)(2,1)S(1)} %shard_map.100), channel_id=1, replica_groups=mesh['role'=4,'zhi'=2,'x'=4,'y'=4,'core'=2] {'x','y'}, dimensions={0} | all-to-all | bytes 2228224 | tf_op jit(solution)/shard_map/all_to_all | solution.py:341
  71.6 0.2 shard_map.101
  71.8 10.7 %all_to_all.22.parts_ref = bf16[8,64,128]{2,1,0:T(8,128)(2,1)S(1)} all-to-all(bf16[8,64,128]{2,1,0:T(8,128)(2,1)S(1)} %shard_map.101), channel_id=1, replica_groups=mesh['role'=4,'zhi'=2,'x'=4,'y'=4,'core'=2] {'role','zhi'}, dimensions={0} | all-to-all | bytes 262144 | tf_op jit(solution)/shard_map/all_to_all | solution.py:343
  82.6 0.7 shard_map.102
Async XLA Ops:
  0.6 25.7 %collective-permute-start.1 = (bf16[2,2,80,7168]{3,2,1,0:T(8,128)(2,1)}, bf16[2,2,80,7168]{3,2,1,0:T(8,128)(2,1)}, u32[]{:S(2)}, u32[]{:S(2)}) collective-permute-start(bf16[2,2,80,7168]{3,2,1,0:T(8,128)(2,1)} %bitcast.6), channel_id=1, source_target_pairs={{0,1},{1,0},{2,3},{3,2},{4,5},{5,4},{6,7},{7,6},{8,9},{9,8},{10,11... | collective-permute-start | bytes 13762568 | tf_op jit(solution)/shard_map/ppermute | solution.py:308
  0.7 25.5 %collective-permute-start.2 = (bf16[2,80,7168]{2,1,0:T(8,128)(2,1)}, bf16[2,80,7168]{2,1,0:T(8,128)(2,1)}, u32[]{:S(2)}, u32[]{:S(2)}) collective-permute-start(bf16[2,80,7168]{2,1,0:T(8,128)(2,1)} %down_hbm.1), channel_id=1, source_target_pairs={{0,1},{1,0},{2,3},{3,2},{4,5},{5,4},{6,7},{7,6},{8,9},{9,8},{10,11... | collective-permute-start | bytes 6881288 | tf_op jit(solution)/shard_map/ppermute | solution.py:308
  1.2 25.0 %collective-permute-start = (bf16[2,1024,512]{2,1,0:T(8,128)(2,1)}, bf16[2,1024,512]{2,1,0:T(8,128)(2,1)}, u32[]{:S(2)}, u32[]{:S(2)}) collective-permute-start(bf16[2,1024,512]{2,1,0:T(8,128)(2,1)} %mine_hbm.1), channel_id=1, source_target_pairs={{0,1},{1,0},{2,3},{3,2},{4,5},{5,4},{6,7},{7,6},{8,9},{9,8},{10,11... | collective-permute-start | bytes 6291464 | tf_op jit(solution)/shard_map/ppermute | solution.py:308
  19.2 22.2 %all-to-all-start.1 = ((bf16[16,224,128]{2,1,0:T(8,128)(2,1)}), bf16[16,224,128]{2,1,0:T(8,128)(2,1)S(1)}, u32[]{:S(2)}, u32[]{:S(2)}) async-start(bf16[16,224,128]{2,1,0:T(8,128)(2,1)} %get-tuple-element.8.after_ref), calls=%async_computation.1 | async-start | bytes 1835008 | tf_op jit(solution)/shard_map/all_to_all | solution.py:303
  41.4 1.6 %copy-start.1 = (bf16[2,2,320,896]{3,2,1,0:T(8,128)(2,1)S(1)}, bf16[2,2,320,896]{3,2,1,0:T(8,128)(2,1)}, u32[]{:S(2)}) copy-start(bf16[2,2,320,896]{3,2,1,0:T(8,128)(2,1)} %get-tuple-element.10.gate_ref) | copy-start | bytes 6881284
  43.1 1.6 %copy-start.2 = (bf16[2,2,320,896]{3,2,1,0:T(8,128)(2,1)S(1)}, bf16[2,2,320,896]{3,2,1,0:T(8,128)(2,1)}, u32[]{:S(2)}) copy-start(bf16[2,2,320,896]{3,2,1,0:T(8,128)(2,1)} %get-tuple-element.9.gate_ref) | copy-start | bytes 6881284
  43.8 3.4 %copy-start = (bf16[4,2,160,896]{3,2,1,0:T(8,128)(2,1)S(1)}, bf16[4,2,160,896]{3,2,1,0:T(8,128)(2,1)}, u32[]{:S(2)}) copy-start(bf16[4,2,160,896]{3,2,1,0:T(8,128)(2,1)} %get-tuple-element.12.down_ref) | copy-start | bytes 6881284
  43.8 3.4 %copy-start.3 = (bf16[32,8,384]{2,1,0:T(8,128)(2,1)S(1)}, bf16[32,8,384]{2,1,0:T(8,128)(2,1)}, u32[]{:S(2)}) copy-start(bf16[32,8,384]{2,1,0:T(8,128)(2,1)} %get-tuple-element.13.attended_ref) | copy-start | bytes 589828
  45.5 1.7 %collective-permute-start.3 = (f32[2,320,128]{2,1,0:T(8,128)S(1)}, f32[2,320,128]{2,1,0:T(8,128)S(1)}, u32[]{:S(2)}, u32[]{:S(2)}) collective-permute-start(f32[2,320,128]{2,1,0:T(8,128)S(1)} %shard_map.99.mine_ref), channel_id=1, source_target_pairs={{0,1},{1,0},{2,3},{3,2},{4,5},{5,4},{6,7},{7,6},{8,9},{9,8},{10,11... | collective-permute-start | bytes 983048 | tf_op jit(solution)/shard_map/ppermute | solution.py:339

commit v3 on v2

--- a/solution.py
+++ b/solution.py
@@ -120,7 +120,7 @@
 
 def local_kernel(
     seq_ref, q_hbm, mine_hbm, theirs_hbm, gate_hbm, got_gate_hbm, down_hbm, got_down_hbm, after_ref,
-    attended_ref, out_g0_hbm, out_g1_hbm, out_d_ref,
+    attended_ref, out_g_hbm, out_d_ref,
     q_ref, cache_ref, in_ref, out_g_ref, cache_sems, in_sems, out_sems,
 ):
     core = lax.axis_index("core")
@@ -138,18 +138,19 @@
                         ref.at[at], cache_ref.at[(k,) + at], cache_sems.at[len(cache_loads)]
                     )
                 )
-                cache_loads[-1].start(priority=i % 2)
+                cache_loads[-1].start()
     sources = [ref.at[e, g] for ref in (gate_hbm, got_gate_hbm) for e in range(2) for g in range(2)]
     sources += [ref.at[e] for ref in (down_hbm, got_down_hbm) for e in range(2)]
     loads = [
         pltpu.make_async_copy(source, in_ref.at[i], in_sems.at[i]) for i, source in enumerate(sources)
     ]
-    for i, load in enumerate(loads):
-        load.start(priority=i % 2)
 
     def wait(k):
         for load in cache_loads[8 * k : 8 * k + 8]:
             load.wait()
+        if k == 1:
+            for load in loads:
+                load.start()
 
     q_load.wait()
     queries = [
@@ -160,12 +161,8 @@
 
     stores = []
     for i in range(8):
-        for piece in range(4):
-            at = (piece, i // 4, pl.ds((i % 4) * units, units))
-            to = (out_g0_hbm, out_g1_hbm)[piece // 2].at[(piece % 2,) + at[1:]]
-            stores.append(
-                pltpu.make_async_copy(out_g_ref.at[at], to, out_sems.at[len(stores)])
-            )
+        at = (i // 4, pl.ds((i % 4) * units, units))
+        stores.append(pltpu.make_async_copy(out_g_ref.at[at], out_g_hbm.at[at], out_sems.at[i]))
     for i, load in enumerate(loads):
         load.wait()
         out = out_g_ref if i < 8 else out_d_ref
@@ -184,32 +181,21 @@
                         for p in range(4)
                         for z in range(2)
                     ]
-                    out[piece, k, row : row + units, :] = jnp.concatenate(parts, axis=1)
-
-        for store in stores[4 * i : 4 * i + 4] if i < 8 else []:
-            store.start()
+                    to = slice(piece * 8 * BLK, (piece + 1) * 8 * BLK)
+                    out[k, row : row + units, to] = jnp.concatenate(parts, axis=1)
+
+        if i < 8:
+            stores[i].start()
     for store in stores:
         store.wait()
 
 
-def up_first_kernel(rows_ref, gate_ref, out_ref):
-    total = 0.0
-    for piece in range(2):
-        rows = rows_ref[4 * piece : 4 * piece + 4].reshape(8 * BLK, ROWS)
-        total += jnp.dot(
-            gate_ref[piece].reshape(-1, 8 * BLK), rows, preferred_element_type=F32
-        )
-    out_ref[...] = total.reshape(out_ref.shape)
-
-
-def up_second_kernel(rows_ref, gate_ref, before_ref, out_ref):
-    total = before_ref[...].reshape(-1, ROWS)
-    for piece in range(2):
-        rows = rows_ref[8 + 4 * piece : 12 + 4 * piece].reshape(8 * BLK, ROWS)
-        total += jnp.dot(
-            gate_ref[piece].reshape(-1, 8 * BLK), rows, preferred_element_type=F32
-        )
-    out_ref[...] = total.reshape(out_ref.shape)
+def up_kernel(rows_ref, gate_ref, out_ref, send_ref):
+    rows = rows_ref[...].reshape(XY * NX, ROWS)
+    for k in range(2):
+        both = jnp.dot(gate_ref[k], rows, preferred_element_type=F32)
+        out_ref[k] = both
+        send_ref[k] = both.astype(BF16)
 
 
 def activate(both, weight_ref, role, units):
@@ -226,13 +212,14 @@
     role = lax.axis_index("role")
     units = mine_ref.shape[1] // 4
     hidden = [
-        activate(mine_ref[k] + theirs_ref[1 - k], weight_ref, role, units) for k in range(2)
+        activate(mine_ref[k] + theirs_ref[1 - k].astype(F32), weight_ref, role, units) for k in range(2)
     ]
     dims = (((0,), (0,)), ((), ()))
     for piece in range(4):
+        cut = slice(piece * 8 * BLK, (piece + 1) * 8 * BLK)
         part = (
-            lax.dot_general(down_ref[piece, 0], hidden[0], dims, preferred_element_type=F32)
-            + lax.dot_general(down_ref[piece, 1], hidden[1], dims, preferred_element_type=F32)
+            lax.dot_general(down_ref[0, :, cut], hidden[0], dims, preferred_element_type=F32)
+            + lax.dot_general(down_ref[1, :, cut], hidden[1], dims, preferred_element_type=F32)
         ).astype(BF16)
         out_ref[4 * piece : 4 * piece + 4, :NX, :] = part.reshape(4, NX, ROWS)
     both = attended_ref[...].astype(F32).reshape(2, XY, 8, 384)
@@ -253,13 +240,11 @@
         norm = jnp.sum(weight, axis=0)
         out = jnp.concatenate([jnp.sum(p * weight, axis=0) for p in pieces[:2]], axis=1) / norm
         head = with_lse(out, top[0] + jnp.log(norm))
-        tail = [head[:, p * 128 : (p + 1) * 128] for p in range(3)] + [jnp.zeros((8, 128), F32)]
-        tail = jnp.concatenate(tail, axis=0)
-        turned = jnp.concatenate(
-            [total[z * BLK : (z + 1) * BLK].T, jnp.zeros((ROWS, 128 - BLK), F32)], axis=1
-        )
+        spare = jnp.concatenate([head[:, 256 : 256 + 128 - BLK], jnp.zeros((24, 128 - BLK), F32)], axis=0)
+        turned = total[z * BLK : (z + 1) * BLK].T
         for r in range(4):
-            both = jnp.concatenate([turned[32 * r : 32 * (r + 1)], tail], axis=0)
+            wide = jnp.concatenate([turned[32 * r : 32 * (r + 1)], spare], axis=1)
+            both = jnp.concatenate([wide, head[:, :128], head[:, 128:256]], axis=0)
             out_ref[2 * r + z] = both.astype(BF16)
 
 
@@ -269,13 +254,13 @@
         total += parts_ref[p, :32].astype(F32)
     ffn_ref[...] = total[:, :BLK].astype(BF16)
     role = lax.axis_index("role")
-    heads = [parts_ref[2 * role + z, 32:].astype(F32) for z in range(2)]
-    lse = [jnp.sum(h[16:24], axis=-1, keepdims=True) for h in heads]
+    heads = [parts_ref[2 * role + z].astype(F32) for z in range(2)]
+    lse = [jnp.sum(h[:8, BLK:], axis=-1, keepdims=True) for h in heads]
     top = jnp.maximum(lse[0], lse[1])
     weight = [jnp.exp(v - top) for v in lse]
     out = [
         (heads[0][half] * weight[0] + heads[1][half] * weight[1]) / (weight[0] + weight[1])
-        for half in (slice(0, 8), slice(8, 16))
+        for half in (slice(32, 40), slice(40, 48))
     ]
     attention_ref[...] = jnp.concatenate(out, axis=1).astype(BF16)
 
@@ -306,13 +291,12 @@
     gate = gate_up.transpose(0, 2, 3, 1)
     units = gate_up.shape[3]
     pairs = [w for a in (cache, gate, down_proj) for w in (a, lax.ppermute(a, "core", swap))]
-    attended, gate_0, gate_1, down_c = call(
+    attended, gate_c, down_c = call(
         local_kernel,
         [
             shape((32, 8, 384), BF16),
-            shape((2, 2, 4 * units, 8 * BLK), BF16),
-            shape((2, 2, 4 * units, 8 * BLK), BF16),
-            shape((4, 2, 2 * units, 8 * BLK), BF16),
+            shape((2, 4 * units, 32 * BLK), BF16),
+            shape((2, 2 * units, 32 * BLK), BF16),
         ],
         (beam_sequence, query, *pairs, packed),
         [SMEM] + [HBM] * 7 + [ANY],
@@ -321,25 +305,27 @@
             pltpu.VMEM((32, 8, 256), BF16),
             pltpu.VMEM((2,) + cache.shape, BF16),
             pltpu.VMEM((12, units, 64 * BLK), BF16),
-            pltpu.VMEM((4, 2, 4 * units, 8 * BLK), BF16),
+            pltpu.VMEM((2, 4 * units, 32 * BLK), BF16),
             pltpu.SemaphoreType.DMA((17,)),
             pltpu.SemaphoreType.DMA((12,)),
-            pltpu.SemaphoreType.DMA((32,)),
+            pltpu.SemaphoreType.DMA((8,)),
         ],
         pl.CostEstimate(flops=1 << 31, bytes_accessed=24 << 20, transcendentals=1 << 19),
-        [VMEM, HBM, HBM, VMEM],
-    )
-
-    first = shape((2, 4 * units, ROWS), F32)
-    first = call(up_first_kernel, first, (gathered, gate_0))
-    first = call(up_second_kernel, first, (gathered, gate_1, first))
+        [VMEM, HBM, VMEM],
+    )
+
+    first, send = call(
+        up_kernel,
+        [shape((2, 4 * units, ROWS), F32), shape((2, 4 * units, ROWS), BF16)],
+        (gathered, gate_c),
+    )
     half = call(
         down_kernel,
         shape((XY, NX + NA, 128), BF16),
-        (first, lax.ppermute(first, "core", swap), weight, down_c, attended),
+        (first, lax.ppermute(send, "core", swap), weight, down_c, attended),
     )
     spread = lax.all_to_all(half, ("x", "y"), 0, 0, tiled=True)
-    partial = call(turn_kernel, shape((8, 64, 128), BF16), (spread,))
+    partial = call(turn_kernel, shape((8, 48, 128), BF16), (spread,))
     ends = lax.all_to_all(partial, ("role", "zhi"), 0, 0, tiled=True)
     attention_out, ffn_out = call(
         last_kernel, [shape((8, 256), BF16), shape((32, BLK), BF16)], (ends,)

time: 83.7 us -> 81.5 us (0.974)
  blocking collectives: 49.3 us -> 47.7 us
  Pallas kernels: 19.2 us -> 17.9 us
  waiting for transfers between devices: 3.59 us -> 4.72 us
    all_to_all x1, waiting for transfers between devices: 1.97 us -> 3.33 us  [shards(): gathered = lax.all_to_all(packed, ('x', 'y'), 0, 0, tiled=True)]
    pallas_call x8 -> x7, Pallas kernels: 19.2 us -> 17.9 us  [call(): pl.pallas_call(kernel, out_shape=out_shape, in_specs=specs or [VMEM] * le...]
    all_to_all x1, blocking collectives: 23.2 us -> 21.8 us  [shards(): spread = lax.all_to_all(half, ('x', 'y'), 0, 0, tiled=True)]
    unnamed x8 -> x6, local copies, waits for them, and re-layouts: 2.53 us -> 2.31 us
  transfers between devices with their start and end apart: 5 -> 5, of which waited for: 2 -> 2; matrix products, arithmetic and copies ran while one was open for 0% -> 0% of each run, Pallas kernels for 19% -> 18%
where the time goes in v3:
time: 81.5 us; the launch traced here: 81.1 us
  blocking collectives  47.7 us (59%)
  Pallas kernels  17.9 us (22%)
  starting transfers between devices  7.82 us (10%)
  waiting for transfers between devices  4.72 us (6%)
  local copies, waits for them, and re-layouts  2.31 us (3%)
    all_to_all x1, blocking collectives, shards(): spread = lax.all_to_all(half, ('x', 'y'), 0, 0, tiled=True)  21.8 us
    pallas_call x7, Pallas kernels, call(): pl.pallas_call(kernel, out_shape=out_shape, in_specs=specs or [VMEM] * le...  17.9 us
    all_to_all x1, blocking collectives, shards(): rows = lax.all_to_all(message, ('role', 'zhi'), 0, 0, tiled=True)  15.4 us
    all_to_all x1, blocking collectives, shards(): ends = lax.all_to_all(partial, ('role', 'zhi'), 0, 0, tiled=True)  10.4 us
    all_to_all x1, starting transfers between devices, shards(): gathered = lax.all_to_all(packed, ('x', 'y'), 0, 0, tiled=True)  7.03 us
    all_to_all x1, waiting for transfers between devices, shards(): gathered = lax.all_to_all(packed, ('x', 'y'), 0, 0, tiled=True)  3.33 us
    unnamed x6, local copies, waits for them, and re-layouts  2.31 us
  transfers between devices with their start and end apart: 5, of which 2 were waited for; matrix products, arithmetic and copies ran while one was open for 0% of the time, Pallas kernels for 18%

profile of v3, /device:TPU:32, one launch (start us, length us, event | category | flops | bytes accessed | tf_op | source)
XLA Modules:
  0.0 81.1 jit_solution(14029511083262540061)
XLA Ops:
  0.6 0.1 collective-permute-start.1
  0.7 0.5 collective-permute-start.2
  1.2 0.1 collective-permute-start
  1.3 1.4 %shard_map.95 = bf16[8,32,128]{2,1,0:T(8,128)(2,1)} custom-call(bf16[32,112]{1,0:T(8,128)(2,1)} %x_hbm.1, s32[3,32]{1,0:T(4,128)} %bitcast.9, f32[3,32]{1,0:T(4,128)} %bitcast.10), custom_call_target="tpu_custom_call" | custom-call | tf_op jit(solution)/shard_map/pallas_call | solution.py:24
  2.8 15.4 %all_to_all.20.rows_ref = bf16[8,32,128]{2,1,0:T(8,128)(2,1)S(1)} all-to-all(bf16[8,32,128]{2,1,0:T(8,128)(2,1)} %shard_map.95), channel_id=1, replica_groups=mesh['role'=4,'zhi'=2,'x'=4,'y'=4,'core'=2] {'role','zhi'}, dimensions={0} | all-to-all | bytes 131072 | tf_op jit(solution)/shard_map/all_to_all | solution.py:286
  18.2 1.1 %shard_map.96 = (bf16[16,224,128]{2,1,0:T(8,128)(2,1)}, f32[8,128]{1,0:T(8,128)S(1)}) custom-call(bf16[8,32,128]{2,1,0:T(8,128)(2,1)S(1)} %all_to_all.20.rows_ref), custom_call_target="tpu_custom_call" | custom-call | tf_op jit(solution)/shard_map/pallas_call | solution.py:24
  19.2 7.0 %all-to-all-start.1 = ((bf16[16,224,128]{2,1,0:T(8,128)(2,1)}), bf16[16,224,128]{2,1,0:T(8,128)(2,1)S(1)}, u32[]{:S(2)}, u32[]{:S(2)}) async-start(bf16[16,224,128]{2,1,0:T(8,128)(2,1)} %get-tuple-element.9.after_ref), calls=%async_computation.1 | async-start | bytes 1835008 | tf_op jit(solution)/shard_map/all_to_all | solution.py:288
  26.3 0.0 collective-permute-done.theirs_hbm
  26.3 0.0 collective-permute-done.2.got_down_hbm
  26.3 0.0 collective-permute-done.1.got_gate_hbm
  26.3 11.8 %shard_map.97 = (bf16[32,8,384]{2,1,0:T(8,128)(2,1)}, bf16[2,320,3584]{2,1,0:T(8,128)(2,1)}, bf16[2,160,3584]{2,1,0:T(8,128)(2,1)}) custom-call(s32[8]{0:T(128)} %seq_ref.1, bf16[32,2,8,256]{3,2,1,0:T(8,128)(2,1)} %bitcast.8, bf16[2,1024,512]{2,1,0:T(8,128)(2,1)} %mine_hbm.1, bf16[2,1024,512]{2,1,0:T(8,128)(2,1)} %collective-permute-done.theirs_hbm, ...), custom_call_target="tpu_custom_call" | custom-call | flops 2147483648 | bytes 25165824 | tf_op jit(solution)/shard_map/pallas_call | solution.py:24
  38.1 3.3 %all-to-all-done.1.rows_ref = bf16[16,224,128]{2,1,0:T(8,128)(2,1)S(1)} async-done(((bf16[16,224,128]{2,1,0:T(8,128)(2,1)}), bf16[16,224,128]{2,1,0:T(8,128)(2,1)S(1)}, u32[]{:S(2)}, u32[]{:S(2)}) %all-to-all-start.1) | async-done | bytes 917536 | tf_op jit(solution)/shard_map/all_to_all | solution.py:288
  41.4 0.0 copy-start
  41.4 2.3 %copy-done = bf16[2,320,3584]{2,1,0:T(8,128)(2,1)S(1)} copy-done((bf16[2,320,3584]{2,1,0:T(8,128)(2,1)S(1)}, bf16[2,320,3584]{2,1,0:T(8,128)(2,1)}, u32[]{:S(2)}) %copy-start) | copy-done | bytes 4587544
  43.7 0.0 copy-start.1
  43.7 0.0 copy-start.2
  43.7 1.3 %shard_map.98 = (f32[2,320,128]{2,1,0:T(8,128)S(1)}, bf16[2,320,128]{2,1,0:T(8,128)(2,1)S(1)}) custom-call(bf16[16,224,128]{2,1,0:T(8,128)(2,1)S(1)} %all-to-all-done.1.rows_ref, bf16[2,320,3584]{2,1,0:T(8,128)(2,1)S(1)} %copy-done), custom_call_target="tpu_custom_call" | custom-call | tf_op jit(solution)/shard_map/pallas_call | solution.py:24
  45.1 0.1 collective-permute-start.3
  45.2 1.4 %collective-permute-done.3.theirs_ref = bf16[2,320,128]{2,1,0:T(8,128)(2,1)S(1)} collective-permute-done((bf16[2,320,128]{2,1,0:T(8,128)(2,1)S(1)}, bf16[2,320,128]{2,1,0:T(8,128)(2,1)S(1)}, u32[]{:S(2)}, u32[]{:S(2)}) %collective-permute-start.3) | collective-permute-done | bytes 163872 | tf_op jit(solution)/shard_map/ppermute | solution.py:325
  46.6 0.0 copy-done.1
  46.6 0.0 copy-done.2
  46.6 1.2 %shard_map.99 = bf16[16,272,128]{2,1,0:T(8,128)(2,1)S(1)} custom-call(f32[2,320,128]{2,1,0:T(8,128)S(1)} %get-tuple-element.11.mine_ref, bf16[2,320,128]{2,1,0:T(8,128)(2,1)S(1)} %collective-permute-done.3.theirs_ref, f32[8,128]{1,0:T(8,128)S(1)} %get-tuple-element.13.weight_ref, bf16[2,160,3584]{2,1,0:T(8,128)(2,1)S(1)} %copy-done.1, ...), custom_call_target="tpu_custom_call" | custom-call | tf_op jit(solution)/shard_map/pallas_call | solution.py:24
  47.8 21.8 %all_to_all.21.parts_ref = bf16[16,272,128]{2,1,0:T(8,128)(2,1)S(1)} all-to-all(bf16[16,272,128]{2,1,0:T(8,128)(2,1)S(1)} %shard_map.99), channel_id=1, replica_groups=mesh['role'=4,'zhi'=2,'x'=4,'y'=4,'core'=2] {'x','y'}, dimensions={0} | all-to-all | bytes 2228224 | tf_op jit(solution)/shard_map/all_to_all | solution.py:327
  69.6 0.3 shard_map.100
  69.9 10.4 %all_to_all.22.parts_ref = bf16[8,48,128]{2,1,0:T(8,128)(2,1)S(1)} all-to-all(bf16[8,48,128]{2,1,0:T(8,128)(2,1)S(1)} %shard_map.100), channel_id=1, replica_groups=mesh['role'=4,'zhi'=2,'x'=4,'y'=4,'core'=2] {'role','zhi'}, dimensions={0} | all-to-all | bytes 196608 | tf_op jit(solution)/shard_map/all_to_all | solution.py:329
  80.4 0.8 shard_map.101
Async XLA Ops:
  0.6 25.7 %collective-permute-start.1 = (bf16[2,2,80,7168]{3,2,1,0:T(8,128)(2,1)}, bf16[2,2,80,7168]{3,2,1,0:T(8,128)(2,1)}, u32[]{:S(2)}, u32[]{:S(2)}) collective-permute-start(bf16[2,2,80,7168]{3,2,1,0:T(8,128)(2,1)} %bitcast.6), channel_id=1, source_target_pairs={{0,1},{1,0},{2,3},{3,2},{4,5},{5,4},{6,7},{7,6},{8,9},{9,8},{10,11... | collective-permute-start | bytes 13762568 | tf_op jit(solution)/shard_map/ppermute | solution.py:293
  0.7 25.6 %collective-permute-start.2 = (bf16[2,80,7168]{2,1,0:T(8,128)(2,1)}, bf16[2,80,7168]{2,1,0:T(8,128)(2,1)}, u32[]{:S(2)}, u32[]{:S(2)}) collective-permute-start(bf16[2,80,7168]{2,1,0:T(8,128)(2,1)} %down_hbm.1), channel_id=1, source_target_pairs={{0,1},{1,0},{2,3},{3,2},{4,5},{5,4},{6,7},{7,6},{8,9},{9,8},{10,11... | collective-permute-start | bytes 6881288 | tf_op jit(solution)/shard_map/ppermute | solution.py:293
  1.2 25.0 %collective-permute-start = (bf16[2,1024,512]{2,1,0:T(8,128)(2,1)}, bf16[2,1024,512]{2,1,0:T(8,128)(2,1)}, u32[]{:S(2)}, u32[]{:S(2)}) collective-permute-start(bf16[2,1024,512]{2,1,0:T(8,128)(2,1)} %mine_hbm.1), channel_id=1, source_target_pairs={{0,1},{1,0},{2,3},{3,2},{4,5},{5,4},{6,7},{7,6},{8,9},{9,8},{10,11... | collective-permute-start | bytes 6291464 | tf_op jit(solution)/shard_map/ppermute | solution.py:293
  19.2 22.2 %all-to-all-start.1 = ((bf16[16,224,128]{2,1,0:T(8,128)(2,1)}), bf16[16,224,128]{2,1,0:T(8,128)(2,1)S(1)}, u32[]{:S(2)}, u32[]{:S(2)}) async-start(bf16[16,224,128]{2,1,0:T(8,128)(2,1)} %get-tuple-element.9.after_ref), calls=%async_computation.1 | async-start | bytes 1835008 | tf_op jit(solution)/shard_map/all_to_all | solution.py:288
  41.4 2.3 %copy-start = (bf16[2,320,3584]{2,1,0:T(8,128)(2,1)S(1)}, bf16[2,320,3584]{2,1,0:T(8,128)(2,1)}, u32[]{:S(2)}) copy-start(bf16[2,320,3584]{2,1,0:T(8,128)(2,1)} %get-tuple-element.10.gate_ref) | copy-start | bytes 13762564
  43.7 2.8 %copy-start.1 = (bf16[2,160,3584]{2,1,0:T(8,128)(2,1)S(1)}, bf16[2,160,3584]{2,1,0:T(8,128)(2,1)}, u32[]{:S(2)}) copy-start(bf16[2,160,3584]{2,1,0:T(8,128)(2,1)} %get-tuple-element.14.down_ref) | copy-start | bytes 6881284
  43.7 2.8 %copy-start.2 = (bf16[32,8,384]{2,1,0:T(8,128)(2,1)S(1)}, bf16[32,8,384]{2,1,0:T(8,128)(2,1)}, u32[]{:S(2)}) copy-start(bf16[32,8,384]{2,1,0:T(8,128)(2,1)} %get-tuple-element.15.attended_ref) | copy-start | bytes 589828
  45.1 1.5 %collective-permute-start.3 = (bf16[2,320,128]{2,1,0:T(8,128)(2,1)S(1)}, bf16[2,320,128]{2,1,0:T(8,128)(2,1)S(1)}, u32[]{:S(2)}, u32[]{:S(2)}) collective-permute-start(bf16[2,320,128]{2,1,0:T(8,128)(2,1)S(1)} %get-tuple-element.12), channel_id=1, source_target_pairs={{0,1},{1,0},{2,3},{3,2},{4,5},{5,4},{6,7},{7,6},{8,9},{9,8},{10,11... | collective-permute-start | bytes 491528 | tf_op jit(solution)/shard_map/ppermute | solution.py:325

commit v4 on v3

--- a/solution.py
+++ b/solution.py
@@ -120,8 +120,8 @@
 
 def local_kernel(
     seq_ref, q_hbm, mine_hbm, theirs_hbm, gate_hbm, got_gate_hbm, down_hbm, got_down_hbm, after_ref,
-    attended_ref, out_g_hbm, out_d_ref,
-    q_ref, cache_ref, in_ref, out_g_ref, cache_sems, in_sems, out_sems,
+    attended_ref, out_g_hbm, out_d_hbm,
+    q_ref, cache_ref, in_ref, out_g_ref, out_d_ref, cache_sems, in_sems, out_sems,
 ):
     core = lax.axis_index("core")
     units = in_ref.shape[1]
@@ -148,9 +148,8 @@
     def wait(k):
         for load in cache_loads[8 * k : 8 * k + 8]:
             load.wait()
-        if k == 1:
-            for load in loads:
-                load.start()
+        for load in loads[:4] if k == 0 else loads[4:]:
+            load.start()
 
     q_load.wait()
     queries = [
@@ -160,42 +159,46 @@
     attend(seq_ref, queries, cache_ref, [lambda: wait(0), lambda: wait(1)], attended_ref)
 
     stores = []
-    for i in range(8):
-        at = (i // 4, pl.ds((i % 4) * units, units))
-        stores.append(pltpu.make_async_copy(out_g_ref.at[at], out_g_hbm.at[at], out_sems.at[i]))
-    for i, load in enumerate(loads):
-        load.wait()
+    for i in range(12):
+        at = pl.ds((i if i < 8 else i - 8) * units, units)
+        src, dst = (out_g_ref, out_g_hbm) if i < 8 else (out_d_ref, out_d_hbm)
+        stores.append(pltpu.make_async_copy(src.at[at], dst.at[at], out_sems.at[i]))
+    lane = lax.broadcasted_iota(jnp.int32, (units, 8 * BLK), 1)
+    even = ((lane // BLK) % 2 == 0).astype(F32).astype(BF16) > 0
+
+    def sort(i):
+        loads[i].wait()
         out = out_g_ref if i < 8 else out_d_ref
-        k, row = (i // 4, (i % 4) * units) if i < 8 else ((i - 8) // 2, (i % 2) * units)
+        row = (i if i < 8 else i - 8) * units
         for parity in range(2):
 
             @pl.when(core == parity)
             def _():
                 for piece in range(4):
-                    wide = [
+                    low, high = (
                         in_ref[i, :, (z * 4 + piece) * 8 * BLK : (z * 4 + piece + 1) * 8 * BLK]
                         for z in range(2)
-                    ]
-                    parts = [
-                        wide[z][:, (2 * p + parity) * BLK : (2 * p + parity + 1) * BLK]
-                        for p in range(4)
-                        for z in range(2)
-                    ]
+                    )
+                    if parity:
+                        low = jnp.concatenate([low[:, BLK:], low[:, :BLK]], axis=1)
+                    else:
+                        high = jnp.concatenate([high[:, -BLK:], high[:, :-BLK]], axis=1)
                     to = slice(piece * 8 * BLK, (piece + 1) * 8 * BLK)
-                    out[k, row : row + units, to] = jnp.concatenate(parts, axis=1)
-
-        if i < 8:
-            stores[i].start()
+                    out[row : row + units, to] = jnp.where(even, low, high)
+
+        stores[i].start()
+
+    for i in range(len(loads)):
+        sort(i)
     for store in stores:
         store.wait()
 
 
 def up_kernel(rows_ref, gate_ref, out_ref, send_ref):
     rows = rows_ref[...].reshape(XY * NX, ROWS)
-    for k in range(2):
-        both = jnp.dot(gate_ref[k], rows, preferred_element_type=F32)
-        out_ref[k] = both
-        send_ref[k] = both.astype(BF16)
+    both = jnp.dot(gate_ref[...], rows, preferred_element_type=F32)
+    out_ref[...] = both
+    send_ref[...] = both.astype(BF16)
 
 
 def activate(both, weight_ref, role, units):
@@ -210,18 +213,28 @@
 
 def down_kernel(mine_ref, theirs_ref, weight_ref, down_ref, attended_ref, out_ref):
     role = lax.axis_index("role")
-    units = mine_ref.shape[1] // 4
-    hidden = [
-        activate(mine_ref[k] + theirs_ref[1 - k].astype(F32), weight_ref, role, units) for k in range(2)
-    ]
-    dims = (((0,), (0,)), ((), ()))
+    rows = mine_ref.shape[0] // 2
+    hidden = jnp.concatenate(
+        [
+            activate(
+                mine_ref[k * rows : (k + 1) * rows]
+                + theirs_ref[(1 - k) * rows : (2 - k) * rows].astype(F32),
+                weight_ref,
+                role,
+                rows // 4,
+            )
+            for k in range(2)
+        ],
+        axis=0,
+    )
     for piece in range(4):
-        cut = slice(piece * 8 * BLK, (piece + 1) * 8 * BLK)
-        part = (
-            lax.dot_general(down_ref[0, :, cut], hidden[0], dims, preferred_element_type=F32)
-            + lax.dot_general(down_ref[1, :, cut], hidden[1], dims, preferred_element_type=F32)
-        ).astype(BF16)
-        out_ref[4 * piece : 4 * piece + 4, :NX, :] = part.reshape(4, NX, ROWS)
+        part = lax.dot_general(
+            down_ref[:, piece * 8 * BLK : (piece + 1) * 8 * BLK],
+            hidden,
+            (((0,), (0,)), ((), ())),
+            preferred_element_type=F32,
+        )
+        out_ref[4 * piece : 4 * piece + 4, :NX, :] = part.astype(BF16).reshape(4, NX, ROWS)
     both = attended_ref[...].astype(F32).reshape(2, XY, 8, 384)
     pieces = [both[z, :, :, p * 128 : (p + 1) * 128] for z in range(2) for p in range(3)]
     out_ref[:, NX:, :] = jnp.concatenate(pieces, axis=1).astype(BF16)
@@ -295,8 +308,8 @@
         local_kernel,
         [
             shape((32, 8, 384), BF16),
-            shape((2, 4 * units, 32 * BLK), BF16),
-            shape((2, 2 * units, 32 * BLK), BF16),
+            shape((8 * units, 32 * BLK), BF16),
+            shape((4 * units, 32 * BLK), BF16),
         ],
         (beam_sequence, query, *pairs, packed),
         [SMEM] + [HBM] * 7 + [ANY],
@@ -305,18 +318,19 @@
             pltpu.VMEM((32, 8, 256), BF16),
             pltpu.VMEM((2,) + cache.shape, BF16),
             pltpu.VMEM((12, units, 64 * BLK), BF16),
-            pltpu.VMEM((2, 4 * units, 32 * BLK), BF16),
+            pltpu.VMEM((8 * units, 32 * BLK), BF16),
+            pltpu.VMEM((4 * units, 32 * BLK), BF16),
             pltpu.SemaphoreType.DMA((17,)),
             pltpu.SemaphoreType.DMA((12,)),
-            pltpu.SemaphoreType.DMA((8,)),
+            pltpu.SemaphoreType.DMA((12,)),
         ],
         pl.CostEstimate(flops=1 << 31, bytes_accessed=24 << 20, transcendentals=1 << 19),
-        [VMEM, HBM, VMEM],
+        [VMEM, HBM, HBM],
     )
 
     first, send = call(
         up_kernel,
-        [shape((2, 4 * units, ROWS), F32), shape((2, 4 * units, ROWS), BF16)],
+        [shape((8 * units, ROWS), F32), shape((8 * units, ROWS), BF16)],
         (gathered, gate_c),
     )
     half = call(

time: 81.5 us -> 80.8 us (level)
  transfers between devices with their start and end apart: 5 -> 5, of which waited for: 2 -> 2; matrix products, arithmetic and copies ran while one was open for 0% -> 0% of each run, Pallas kernels for 18% -> 17%
where the time goes in v4:
time: 80.8 us; the launch traced here: 80.4 us
  blocking collectives  47.2 us (58%)
  Pallas kernels  17.1 us (21%)
  starting transfers between devices  7.82 us (10%)
  waiting for transfers between devices  5.26 us (7%)
  local copies, waits for them, and re-layouts  2.31 us (3%)
    all_to_all x1, blocking collectives, shards(): spread = lax.all_to_all(half, ('x', 'y'), 0, 0, tiled=True)  21.5 us
    pallas_call x7, Pallas kernels, call(): pl.pallas_call(kernel, out_shape=out_shape, in_specs=specs or [VMEM] * le...  17.1 us
    all_to_all x1, blocking collectives, shards(): rows = lax.all_to_all(message, ('role', 'zhi'), 0, 0, tiled=True)  15.4 us
    all_to_all x1, blocking collectives, shards(): ends = lax.all_to_all(partial, ('role', 'zhi'), 0, 0, tiled=True)  10.3 us
    all_to_all x1, starting transfers between devices, shards(): gathered = lax.all_to_all(packed, ('x', 'y'), 0, 0, tiled=True)  7.03 us
    all_to_all x1, waiting for transfers between devices, shards(): gathered = lax.all_to_all(packed, ('x', 'y'), 0, 0, tiled=True)  3.87 us
    unnamed x6, local copies, waits for them, and re-layouts  2.31 us
  transfers between devices with their start and end apart: 5, of which 2 were waited for; matrix products, arithmetic and copies ran while one was open for 0% of the time, Pallas kernels for 17%

profile of v4, /device:TPU:32, one launch (start us, length us, event | category | flops | bytes accessed | tf_op | source)
XLA Modules:
  0.0 80.4 jit_solution(3906369884529869499)
XLA Ops:
  0.6 0.1 collective-permute-start.1
  0.7 0.5 collective-permute-start.2
  1.2 0.1 collective-permute-start
  1.3 1.4 %shard_map.95 = bf16[8,32,128]{2,1,0:T(8,128)(2,1)} custom-call(bf16[32,112]{1,0:T(8,128)(2,1)} %x_hbm.1, s32[3,32]{1,0:T(4,128)} %bitcast.9, f32[3,32]{1,0:T(4,128)} %bitcast.10), custom_call_target="tpu_custom_call" | custom-call | tf_op jit(solution)/shard_map/pallas_call | solution.py:24
  2.8 15.4 %all_to_all.20.rows_ref = bf16[8,32,128]{2,1,0:T(8,128)(2,1)S(1)} all-to-all(bf16[8,32,128]{2,1,0:T(8,128)(2,1)} %shard_map.95), channel_id=1, replica_groups=mesh['role'=4,'zhi'=2,'x'=4,'y'=4,'core'=2] {'role','zhi'}, dimensions={0} | all-to-all | bytes 131072 | tf_op jit(solution)/shard_map/all_to_all | solution.py:299
  18.2 1.1 %shard_map.96 = (bf16[16,224,128]{2,1,0:T(8,128)(2,1)}, f32[8,128]{1,0:T(8,128)S(1)}) custom-call(bf16[8,32,128]{2,1,0:T(8,128)(2,1)S(1)} %all_to_all.20.rows_ref), custom_call_target="tpu_custom_call" | custom-call | tf_op jit(solution)/shard_map/pallas_call | solution.py:24
  19.2 7.0 %all-to-all-start.1 = ((bf16[16,224,128]{2,1,0:T(8,128)(2,1)}), bf16[16,224,128]{2,1,0:T(8,128)(2,1)S(1)}, u32[]{:S(2)}, u32[]{:S(2)}) async-start(bf16[16,224,128]{2,1,0:T(8,128)(2,1)} %get-tuple-element.9.after_ref), calls=%async_computation.1 | async-start | bytes 1835008 | tf_op jit(solution)/shard_map/all_to_all | solution.py:301
  26.3 0.0 collective-permute-done.theirs_hbm
  26.3 0.0 collective-permute-done.2.got_down_hbm
  26.3 0.0 collective-permute-done.1.got_gate_hbm
  26.3 11.2 %shard_map.97 = (bf16[32,8,384]{2,1,0:T(8,128)(2,1)}, bf16[640,3584]{1,0:T(8,128)(2,1)}, bf16[320,3584]{1,0:T(8,128)(2,1)}) custom-call(s32[8]{0:T(128)} %seq_ref.1, bf16[32,2,8,256]{3,2,1,0:T(8,128)(2,1)} %bitcast.8, bf16[2,1024,512]{2,1,0:T(8,128)(2,1)} %mine_hbm.1, bf16[2,1024,512]{2,1,0:T(8,128)(2,1)} %collective-permute-done.theirs_hbm, ...), custom_call_target="tpu_custom_call" | custom-call | flops 2147483648 | bytes 25165824 | tf_op jit(solution)/shard_map/pallas_call | solution.py:24
  37.6 3.9 %all-to-all-done.1.rows_ref = bf16[16,224,128]{2,1,0:T(8,128)(2,1)S(1)} async-done(((bf16[16,224,128]{2,1,0:T(8,128)(2,1)}), bf16[16,224,128]{2,1,0:T(8,128)(2,1)S(1)}, u32[]{:S(2)}, u32[]{:S(2)}) %all-to-all-start.1) | async-done | bytes 917536 | tf_op jit(solution)/shard_map/all_to_all | solution.py:301
  41.4 0.0 copy-start
  41.4 2.3 %copy-done = bf16[640,3584]{1,0:T(8,128)(2,1)S(1)} copy-done((bf16[640,3584]{1,0:T(8,128)(2,1)S(1)}, bf16[640,3584]{1,0:T(8,128)(2,1)}, u32[]{:S(2)}) %copy-start) | copy-done | bytes 4587544
  43.7 0.0 copy-start.1
  43.7 0.0 copy-start.2
  43.7 1.4 %shard_map.98 = (f32[640,128]{1,0:T(8,128)S(1)}, bf16[640,128]{1,0:T(8,128)(2,1)S(1)}) custom-call(bf16[16,224,128]{2,1,0:T(8,128)(2,1)S(1)} %all-to-all-done.1.rows_ref, bf16[640,3584]{1,0:T(8,128)(2,1)S(1)} %copy-done), custom_call_target="tpu_custom_call" | custom-call | tf_op jit(solution)/shard_map/pallas_call | solution.py:24
  45.1 0.1 collective-permute-start.3
  45.2 1.4 %collective-permute-done.3.theirs_ref = bf16[640,128]{1,0:T(8,128)(2,1)S(1)} collective-permute-done((bf16[640,128]{1,0:T(8,128)(2,1)S(1)}, bf16[640,128]{1,0:T(8,128)(2,1)S(1)}, u32[]{:S(2)}, u32[]{:S(2)}) %collective-permute-start.3) | collective-permute-done | bytes 163872 | tf_op jit(solution)/shard_map/ppermute | solution.py:339
  46.6 0.0 copy-done.1
  46.6 0.0 copy-done.2
  46.6 1.0 %shard_map.99 = bf16[16,272,128]{2,1,0:T(8,128)(2,1)S(1)} custom-call(f32[640,128]{1,0:T(8,128)S(1)} %get-tuple-element.11.mine_ref, bf16[640,128]{1,0:T(8,128)(2,1)S(1)} %collective-permute-done.3.theirs_ref, f32[8,128]{1,0:T(8,128)S(1)} %get-tuple-element.13.weight_ref, bf16[320,3584]{1,0:T(8,128)(2,1)S(1)} %copy-done.1, bf16[32,8,384]{2,1,0:T(8,128)(2,1)S(1)} %copy-done.2), custom_call_target="tpu_custom_call" | custom-call | tf_op jit(solution)/shard_map/pallas_call | solution.py:24
  47.5 21.5 %all_to_all.21.parts_ref = bf16[16,272,128]{2,1,0:T(8,128)(2,1)S(1)} all-to-all(bf16[16,272,128]{2,1,0:T(8,128)(2,1)S(1)} %shard_map.99), channel_id=1, replica_groups=mesh['role'=4,'zhi'=2,'x'=4,'y'=4,'core'=2] {'x','y'}, dimensions={0} | all-to-all | bytes 2228224 | tf_op jit(solution)/shard_map/all_to_all | solution.py:341
  69.0 0.3 shard_map.100
  69.3 10.3 %all_to_all.22.parts_ref = bf16[8,48,128]{2,1,0:T(8,128)(2,1)S(1)} all-to-all(bf16[8,48,128]{2,1,0:T(8,128)(2,1)S(1)} %shard_map.100), channel_id=1, replica_groups=mesh['role'=4,'zhi'=2,'x'=4,'y'=4,'core'=2] {'role','zhi'}, dimensions={0} | all-to-all | bytes 196608 | tf_op jit(solution)/shard_map/all_to_all | solution.py:343
  79.6 0.8 shard_map.101
Async XLA Ops:
  0.6 25.7 %collective-permute-start.1 = (bf16[2,2,80,7168]{3,2,1,0:T(8,128)(2,1)}, bf16[2,2,80,7168]{3,2,1,0:T(8,128)(2,1)}, u32[]{:S(2)}, u32[]{:S(2)}) collective-permute-start(bf16[2,2,80,7168]{3,2,1,0:T(8,128)(2,1)} %bitcast.6), channel_id=1, source_target_pairs={{0,1},{1,0},{2,3},{3,2},{4,5},{5,4},{6,7},{7,6},{8,9},{9,8},{10,11... | collective-permute-start | bytes 13762568 | tf_op jit(solution)/shard_map/ppermute | solution.py:306
  0.7 25.6 %collective-permute-start.2 = (bf16[2,80,7168]{2,1,0:T(8,128)(2,1)}, bf16[2,80,7168]{2,1,0:T(8,128)(2,1)}, u32[]{:S(2)}, u32[]{:S(2)}) collective-permute-start(bf16[2,80,7168]{2,1,0:T(8,128)(2,1)} %down_hbm.1), channel_id=1, source_target_pairs={{0,1},{1,0},{2,3},{3,2},{4,5},{5,4},{6,7},{7,6},{8,9},{9,8},{10,11... | collective-permute-start | bytes 6881288 | tf_op jit(solution)/shard_map/ppermute | solution.py:306
  1.2 25.0 %collective-permute-start = (bf16[2,1024,512]{2,1,0:T(8,128)(2,1)}, bf16[2,1024,512]{2,1,0:T(8,128)(2,1)}, u32[]{:S(2)}, u32[]{:S(2)}) collective-permute-start(bf16[2,1024,512]{2,1,0:T(8,128)(2,1)} %mine_hbm.1), channel_id=1, source_target_pairs={{0,1},{1,0},{2,3},{3,2},{4,5},{5,4},{6,7},{7,6},{8,9},{9,8},{10,11... | collective-permute-start | bytes 6291464 | tf_op jit(solution)/shard_map/ppermute | solution.py:306
  19.2 22.2 %all-to-all-start.1 = ((bf16[16,224,128]{2,1,0:T(8,128)(2,1)}), bf16[16,224,128]{2,1,0:T(8,128)(2,1)S(1)}, u32[]{:S(2)}, u32[]{:S(2)}) async-start(bf16[16,224,128]{2,1,0:T(8,128)(2,1)} %get-tuple-element.9.after_ref), calls=%async_computation.1 | async-start | bytes 1835008 | tf_op jit(solution)/shard_map/all_to_all | solution.py:301
  41.4 2.3 %copy-start = (bf16[640,3584]{1,0:T(8,128)(2,1)S(1)}, bf16[640,3584]{1,0:T(8,128)(2,1)}, u32[]{:S(2)}) copy-start(bf16[640,3584]{1,0:T(8,128)(2,1)} %get-tuple-element.10.gate_ref) | copy-start | bytes 13762564
  43.7 2.8 %copy-start.1 = (bf16[320,3584]{1,0:T(8,128)(2,1)S(1)}, bf16[320,3584]{1,0:T(8,128)(2,1)}, u32[]{:S(2)}) copy-start(bf16[320,3584]{1,0:T(8,128)(2,1)} %get-tuple-element.14.down_ref) | copy-start | bytes 6881284
  43.7 2.8 %copy-start.2 = (bf16[32,8,384]{2,1,0:T(8,128)(2,1)S(1)}, bf16[32,8,384]{2,1,0:T(8,128)(2,1)}, u32[]{:S(2)}) copy-start(bf16[32,8,384]{2,1,0:T(8,128)(2,1)} %get-tuple-element.15.attended_ref) | copy-start | bytes 589828
  45.1 1.5 %collective-permute-start.3 = (bf16[640,128]{1,0:T(8,128)(2,1)S(1)}, bf16[640,128]{1,0:T(8,128)(2,1)S(1)}, u32[]{:S(2)}, u32[]{:S(2)}) collective-permute-start(bf16[640,128]{1,0:T(8,128)(2,1)S(1)} %get-tuple-element.12), channel_id=1, source_target_pairs={{0,1},{1,0},{2,3},{3,2},{4,5},{5,4},{6,7},{7,6},{8,9},{9,8},{10,11... | collective-permute-start | bytes 491528 | tf_op jit(solution)/shard_map/ppermute | solution.py:339

commit v5 on v4

--- a/solution.py
+++ b/solution.py
@@ -16,7 +16,7 @@
 BLK = 112
 ROWS = 128
 NX = 2 * BLK
-NA = 48
+NA = 40
 
 
 def call(kernel, out_shape, args, specs=None, limit=16 << 20, scratch=(), cost=None, outs=None):
@@ -38,11 +38,14 @@
     return hi, mid, (v - hi) - mid
 
 
+def lse_tile(lse, first=0):
+    hi, mid, lo = split3(lse)
+    lane = lax.broadcasted_iota(jnp.int32, (lse.shape[0], 128), 1) - first
+    return jnp.where(lane == 0, hi, jnp.where(lane == 1, mid, jnp.where(lane == 2, lo, 0.0)))
+
+
 def with_lse(out, lse):
-    hi, mid, lo = split3(lse)
-    lane = lax.broadcasted_iota(jnp.int32, (out.shape[0], 128), 1)
-    tail = jnp.where(lane == 0, hi, jnp.where(lane == 1, mid, jnp.where(lane == 2, lo, 0.0)))
-    return jnp.concatenate([out, tail], axis=1)
+    return jnp.concatenate([out, lse_tile(lse)], axis=1)
 
 
 def lse_of(part):
@@ -85,78 +88,79 @@
             out_ref[p, z * BLK : (z + 1) * BLK, :] = features
 
 
-def attend(seq_ref, queries, caches, waits, out_ref):
-    steps = len(queries)
-    rows = queries[0].shape[0]
+def attend(seq_ref, q_ref, cache, outs):
+    core = lax.axis_index("core")
+    chunk = 16
+    rows = chunk * 8
     place = lax.broadcasted_iota(jnp.int32, (rows, 1), 0) % 8
     pick = jnp.zeros((rows, 1), jnp.int32)
     for r in range(8):
         pick = jnp.where(place == r, seq_ref[r], pick)
     second = pick == 1
     dims = (((1,), (1,)), ((), ()))
-    scores = [[] for _ in range(steps)]
-    for k in range(2):
-        waits[k]()
-        for step in range(steps):
+    for side, out_ref in enumerate(outs):
+        for step in range(q_ref.shape[0] // chunk):
+            at = slice(step * chunk, (step + 1) * chunk)
+            query = q_ref[at, core if side == 0 else 1 - core]
+            query = query.astype(F32).reshape(rows, 256).astype(BF16)
             both = [
-                lax.dot_general(
-                    queries[step], caches[k, s, :, :256], dims, preferred_element_type=F32
-                )
+                lax.dot_general(query, cache[s, :, :256], dims, preferred_element_type=F32)
                 for s in range(2)
             ]
-            scores[step].append(jnp.where(second, both[1], both[0]) * (256 ** -0.5))
-    for step in range(steps):
-        top = jnp.maximum(*(jnp.max(v, axis=1, keepdims=True) for v in scores[step]))
-        total, summed = 0.0, 0.0
-        for k in range(2):
-            expo = jnp.exp(scores[step][k] - top)
-            total += jnp.sum(expo, axis=1, keepdims=True)
+            scores = jnp.where(second, both[1], both[0]) * (256 ** -0.5)
+            top = jnp.max(scores, axis=1, keepdims=True)
+            expo = jnp.exp(scores - top)
+            total = jnp.sum(expo, axis=1, keepdims=True)
+            summed = 0.0
             for s in range(2):
                 part = jnp.where(second == (s == 1), expo, 0.0).astype(BF16)
-                summed += jnp.dot(part, caches[k, s, :, 256:], preferred_element_type=F32)
-        both = with_lse(summed / total, top + jnp.log(total)).reshape(rows // 8, 8, 384)
-        out_ref[step * (rows // 8) : (step + 1) * (rows // 8)] = both.astype(BF16)
+                summed += jnp.dot(part, cache[s, :, 256:], preferred_element_type=F32)
+            both = with_lse(summed / total, top + jnp.log(total)).reshape(chunk, 8, 384)
+            out_ref[at] = both.astype(BF16)
+
+
+def pair(first, second):
+    lse_a, lse_b = lse_of(first), lse_of(second)
+    top = jnp.maximum(lse_a, lse_b)
+    wa, wb = jnp.exp(lse_a - top), jnp.exp(lse_b - top)
+    total = wa + wb
+    out = (first[..., :256] * wa + second[..., :256] * wb) / total
+    return out, top + jnp.log(total)
 
 
 def local_kernel(
-    seq_ref, q_hbm, mine_hbm, theirs_hbm, gate_hbm, got_gate_hbm, down_hbm, got_down_hbm, after_ref,
-    attended_ref, out_g_hbm, out_d_hbm,
+    seq_ref, q_hbm, cache_hbm, gate_hbm, got_gate_hbm, down_hbm, got_down_hbm, after_ref,
+    keep_ref, give_ref, out_g_hbm, out_d_hbm,
     q_ref, cache_ref, in_ref, out_g_ref, out_d_ref, cache_sems, in_sems, out_sems,
 ):
     core = lax.axis_index("core")
     units = in_ref.shape[1]
-    positions = cache_ref.shape[2] // 4
-    q_load = pltpu.make_async_copy(q_hbm.at[:, core], q_ref, cache_sems.at[16])
+    positions = cache_ref.shape[1] // 4
+    q_load = pltpu.make_async_copy(q_hbm, q_ref, cache_sems.at[8])
     q_load.start()
     cache_loads = []
-    for k, ref in enumerate((mine_hbm, theirs_hbm)):
-        for s in range(2):
-            for i in range(4):
-                at = (s, pl.ds(i * positions, positions))
-                cache_loads.append(
-                    pltpu.make_async_copy(
-                        ref.at[at], cache_ref.at[(k,) + at], cache_sems.at[len(cache_loads)]
-                    )
+    for s in range(2):
+        for i in range(4):
+            at = (s, pl.ds(i * positions, positions))
+            cache_loads.append(
+                pltpu.make_async_copy(
+                    cache_hbm.at[at], cache_ref.at[at], cache_sems.at[len(cache_loads)]
                 )
-                cache_loads[-1].start()
+            )
+            cache_loads[-1].start()
     sources = [ref.at[e, g] for ref in (gate_hbm, got_gate_hbm) for e in range(2) for g in range(2)]
     sources += [ref.at[e] for ref in (down_hbm, got_down_hbm) for e in range(2)]
     loads = [
         pltpu.make_async_copy(source, in_ref.at[i], in_sems.at[i]) for i, source in enumerate(sources)
     ]
-
-    def wait(k):
-        for load in cache_loads[8 * k : 8 * k + 8]:
-            load.wait()
-        for load in loads[:4] if k == 0 else loads[4:]:
-            load.start()
-
+    for load in loads[:4]:
+        load.start()
     q_load.wait()
-    queries = [
-        q_ref[step * 16 : (step + 1) * 16].astype(F32).reshape(128, 256).astype(BF16)
-        for step in range(2)
-    ]
-    attend(seq_ref, queries, cache_ref, [lambda: wait(0), lambda: wait(1)], attended_ref)
+    for load in cache_loads:
+        load.wait()
+    for load in loads[4:]:
+        load.start()
+    attend(seq_ref, q_ref, cache_ref, (keep_ref, give_ref))
 
     stores = []
     for i in range(12):
@@ -211,7 +215,9 @@
     return jnp.concatenate(hidden, axis=0)
 
 
-def down_kernel(mine_ref, theirs_ref, weight_ref, down_ref, attended_ref, out_ref):
+def down_kernel(
+    mine_ref, theirs_ref, weight_ref, down_ref, attended_ref, their_attended_ref, out_ref
+):
     role = lax.axis_index("role")
     rows = mine_ref.shape[0] // 2
     hidden = jnp.concatenate(
@@ -235,8 +241,16 @@
             preferred_element_type=F32,
         )
         out_ref[4 * piece : 4 * piece + 4, :NX, :] = part.astype(BF16).reshape(4, NX, ROWS)
-    both = attended_ref[...].astype(F32).reshape(2, XY, 8, 384)
-    pieces = [both[z, :, :, p * 128 : (p + 1) * 128] for z in range(2) for p in range(3)]
+    out, lse = pair(
+        attended_ref[...].astype(F32).reshape(256, 384),
+        their_attended_ref[...].astype(F32).reshape(256, 384),
+    )
+    half = XY * 8
+    pieces = [
+        out[z * half : (z + 1) * half, p * 128 : (p + 1) * 128] for z in range(2) for p in range(2)
+    ]
+    pieces.append(lse_tile(lse[:half]) + lse_tile(lse[half:], 3))
+    pieces = [piece.reshape(XY, 8, 128) for piece in pieces]
     out_ref[:, NX:, :] = jnp.concatenate(pieces, axis=1).astype(BF16)
 
 
@@ -246,12 +260,12 @@
         total += parts_ref[p, :NX].astype(F32)
     parts = parts_ref[:, NX:, :].astype(F32)
     for z in range(2):
-        pieces = [parts[:, (z * 3 + p) * 8 : (z * 3 + p + 1) * 8, :] for p in range(3)]
-        lse = jnp.sum(pieces[2], axis=-1, keepdims=True)
+        pieces = [parts[:, (z * 2 + p) * 8 : (z * 2 + p + 1) * 8, :] for p in range(2)]
+        lse = jnp.sum(parts[:, 32:, 3 * z : 3 * z + 3], axis=-1, keepdims=True)
         top = jnp.max(lse, axis=0, keepdims=True)
         weight = jnp.exp(lse - top)
         norm = jnp.sum(weight, axis=0)
-        out = jnp.concatenate([jnp.sum(p * weight, axis=0) for p in pieces[:2]], axis=1) / norm
+        out = jnp.concatenate([jnp.sum(p * weight, axis=0) for p in pieces], axis=1) / norm
         head = with_lse(out, top[0] + jnp.log(norm))
         spare = jnp.concatenate([head[:, 256 : 256 + 128 - BLK], jnp.zeros((24, 128 - BLK), F32)], axis=0)
         turned = total[z * BLK : (z + 1) * BLK].T
@@ -303,29 +317,30 @@
     query = queries.reshape(8, 32, 2, 256).transpose(1, 2, 0, 3)
     gate = gate_up.transpose(0, 2, 3, 1)
     units = gate_up.shape[3]
-    pairs = [w for a in (cache, gate, down_proj) for w in (a, lax.ppermute(a, "core", swap))]
-    attended, gate_c, down_c = call(
+    pairs = [w for a in (gate, down_proj) for w in (a, lax.ppermute(a, "core", swap))]
+    attended, give, gate_c, down_c = call(
         local_kernel,
         [
+            shape((32, 8, 384), BF16),
             shape((32, 8, 384), BF16),
             shape((8 * units, 32 * BLK), BF16),
             shape((4 * units, 32 * BLK), BF16),
         ],
-        (beam_sequence, query, *pairs, packed),
-        [SMEM] + [HBM] * 7 + [ANY],
+        (beam_sequence, query, cache, *pairs, packed),
+        [SMEM] + [HBM] * 6 + [ANY],
         FULL,
         [
-            pltpu.VMEM((32, 8, 256), BF16),
-            pltpu.VMEM((2,) + cache.shape, BF16),
+            pltpu.VMEM((32, 2, 8, 256), BF16),
+            pltpu.VMEM(cache.shape, BF16),
             pltpu.VMEM((12, units, 64 * BLK), BF16),
             pltpu.VMEM((8 * units, 32 * BLK), BF16),
             pltpu.VMEM((4 * units, 32 * BLK), BF16),
-            pltpu.SemaphoreType.DMA((17,)),
+            pltpu.SemaphoreType.DMA((9,)),
             pltpu.SemaphoreType.DMA((12,)),
             pltpu.SemaphoreType.DMA((12,)),
         ],
         pl.CostEstimate(flops=1 << 31, bytes_accessed=24 << 20, transcendentals=1 << 19),
-        [VMEM, HBM, HBM],
+        [VMEM, VMEM, HBM, HBM],
     )
 
     first, send = call(
@@ -336,7 +351,7 @@
     half = call(
         down_kernel,
         shape((XY, NX + NA, 128), BF16),
-        (first, lax.ppermute(send, "core", swap), weight, down_c, attended),
+        (first, lax.ppermute(send, "core", swap), weight, down_c, attended, lax.ppermute(give, "core", swap)),
     )
     spread = lax.all_to_all(half, ("x", "y"), 0, 0, tiled=True)
     partial = call(turn_kernel, shape((8, 48, 128), BF16), (spread,))

time: 80.8 us -> 80.6 us (level)
  transfers between devices with their start and end apart: 5 -> 5, of which waited for: 2 -> 2; matrix products, arithmetic and copies ran while one was open for 0% -> 0% of each run, Pallas kernels for 17% -> 18%
where the time goes in v5:
time: 80.6 us; the launch traced here: 80.2 us
  blocking collectives  47.3 us (59%)
  Pallas kernels  16.8 us (21%)
  starting transfers between devices  7.81 us (10%)
  waiting for transfers between devices  5.22 us (6%)
  local copies, waits for them, and re-layouts  2.31 us (3%)
    all_to_all x1, blocking collectives, shards(): spread = lax.all_to_all(half, ('x', 'y'), 0, 0, tiled=True)  21.5 us
    pallas_call x7, Pallas kernels, call(): pl.pallas_call(kernel, out_shape=out_shape, in_specs=specs or [VMEM] * le...  16.8 us
    all_to_all x1, blocking collectives, shards(): rows = lax.all_to_all(message, ('role', 'zhi'), 0, 0, tiled=True)  15.4 us
    all_to_all x1, blocking collectives, shards(): ends = lax.all_to_all(partial, ('role', 'zhi'), 0, 0, tiled=True)  10.4 us
    all_to_all x1, starting transfers between devices, shards(): gathered = lax.all_to_all(packed, ('x', 'y'), 0, 0, tiled=True)  7.03 us
    all_to_all x1, waiting for transfers between devices, shards(): gathered = lax.all_to_all(packed, ('x', 'y'), 0, 0, tiled=True)  3.83 us
    unnamed x6, local copies, waits for them, and re-layouts  2.31 us
  transfers between devices with their start and end apart: 5, of which 2 were waited for; matrix products, arithmetic and copies ran while one was open for 0% of the time, Pallas kernels for 18%

profile of v5, /device:TPU:32, one launch (start us, length us, event | category | flops | bytes accessed | tf_op | source)
XLA Modules:
  0.0 80.2 jit_solution(15752754354157981612)
XLA Ops:
  0.6 0.1 collective-permute-start
  0.7 0.5 collective-permute-start.1
  1.2 1.4 %shard_map.95 = bf16[8,32,128]{2,1,0:T(8,128)(2,1)} custom-call(bf16[32,112]{1,0:T(8,128)(2,1)} %x_hbm.1, s32[3,32]{1,0:T(4,128)} %bitcast.9, f32[3,32]{1,0:T(4,128)} %bitcast.10), custom_call_target="tpu_custom_call" | custom-call | tf_op jit(solution)/shard_map/pallas_call | solution.py:24
  2.7 15.4 %all_to_all.20.rows_ref = bf16[8,32,128]{2,1,0:T(8,128)(2,1)S(1)} all-to-all(bf16[8,32,128]{2,1,0:T(8,128)(2,1)} %shard_map.95), channel_id=1, replica_groups=mesh['role'=4,'zhi'=2,'x'=4,'y'=4,'core'=2] {'role','zhi'}, dimensions={0} | all-to-all | bytes 131072 | tf_op jit(solution)/shard_map/all_to_all | solution.py:313
  18.1 1.1 %shard_map.96 = (bf16[16,224,128]{2,1,0:T(8,128)(2,1)}, f32[8,128]{1,0:T(8,128)S(1)}) custom-call(bf16[8,32,128]{2,1,0:T(8,128)(2,1)S(1)} %all_to_all.20.rows_ref), custom_call_target="tpu_custom_call" | custom-call | tf_op jit(solution)/shard_map/pallas_call | solution.py:24
  19.1 7.0 %all-to-all-start.1 = ((bf16[16,224,128]{2,1,0:T(8,128)(2,1)}), bf16[16,224,128]{2,1,0:T(8,128)(2,1)S(1)}, u32[]{:S(2)}, u32[]{:S(2)}) async-start(bf16[16,224,128]{2,1,0:T(8,128)(2,1)} %get-tuple-element.10.after_ref), calls=%async_computation.1 | async-start | bytes 1835008 | tf_op jit(solution)/shard_map/all_to_all | solution.py:315
  26.2 0.0 collective-permute-done.1.got_down_hbm
  26.2 0.0 collective-permute-done.got_gate_hbm
  26.2 10.9 %shard_map.97 = (bf16[32,8,384]{2,1,0:T(8,128)(2,1)}, bf16[32,8,384]{2,1,0:T(8,128)(2,1)}, bf16[640,3584]{1,0:T(8,128)(2,1)}, bf16[320,3584]{1,0:T(8,128)(2,1)}) custom-call(s32[8]{0:T(128)} %seq_ref.1, bf16[32,2,8,256]{3,2,1,0:T(8,128)(2,1)} %bitcast.8, bf16[2,1024,512]{2,1,0:T(8,128)(2,1)} %cache_hbm.1, bf16[2,2,80,7168]{3,2,1,0:T(8,128)(2,1)} %bitcast.7, ...), custom_call_target="tpu_custom_call" | custom-call | flops 2147483648 | bytes 25165824 | tf_op jit(solution)/shard_map/pallas_call | solution.py:24
  37.1 0.1 collective-permute-start.3
  37.2 3.8 %all-to-all-done.1.rows_ref = bf16[16,224,128]{2,1,0:T(8,128)(2,1)S(1)} async-done(((bf16[16,224,128]{2,1,0:T(8,128)(2,1)}), bf16[16,224,128]{2,1,0:T(8,128)(2,1)S(1)}, u32[]{:S(2)}, u32[]{:S(2)}) %all-to-all-start.1) | async-done | bytes 917536 | tf_op jit(solution)/shard_map/all_to_all | solution.py:315
  41.0 0.0 copy-start
  41.0 2.3 %copy-done = bf16[640,3584]{1,0:T(8,128)(2,1)S(1)} copy-done((bf16[640,3584]{1,0:T(8,128)(2,1)S(1)}, bf16[640,3584]{1,0:T(8,128)(2,1)}, u32[]{:S(2)}) %copy-start) | copy-done | bytes 4587544
  43.3 0.0 copy-start.1
  43.3 0.0 copy-start.2
  43.3 1.3 %shard_map.98 = (f32[640,128]{1,0:T(8,128)S(1)}, bf16[640,128]{1,0:T(8,128)(2,1)S(1)}) custom-call(bf16[16,224,128]{2,1,0:T(8,128)(2,1)S(1)} %all-to-all-done.1.rows_ref, bf16[640,3584]{1,0:T(8,128)(2,1)S(1)} %copy-done), custom_call_target="tpu_custom_call" | custom-call | tf_op jit(solution)/shard_map/pallas_call | solution.py:24
  44.7 0.1 collective-permute-start.2
  44.8 1.4 %collective-permute-done.2.theirs_ref = bf16[640,128]{1,0:T(8,128)(2,1)S(1)} collective-permute-done((bf16[640,128]{1,0:T(8,128)(2,1)S(1)}, bf16[640,128]{1,0:T(8,128)(2,1)S(1)}, u32[]{:S(2)}, u32[]{:S(2)}) %collective-permute-start.2) | collective-permute-done | bytes 163872 | tf_op jit(solution)/shard_map/ppermute | solution.py:354
  46.1 0.0 collective-permute-done.3.their_attended_ref
  46.1 0.0 copy-done.1
  46.1 0.0 copy-done.2
  46.1 1.0 %shard_map.99 = bf16[16,264,128]{2,1,0:T(8,128)(2,1)S(1)} custom-call(f32[640,128]{1,0:T(8,128)S(1)} %get-tuple-element.12.mine_ref, bf16[640,128]{1,0:T(8,128)(2,1)S(1)} %collective-permute-done.2.theirs_ref, f32[8,128]{1,0:T(8,128)S(1)} %get-tuple-element.14.weight_ref, bf16[320,3584]{1,0:T(8,128)(2,1)S(1)} %copy-done.1, ...), custom_call_target="tpu_custom_call" | custom-call | tf_op jit(solution)/shard_map/pallas_call | solution.py:24
  47.2 21.5 %all_to_all.21.parts_ref = bf16[16,264,128]{2,1,0:T(8,128)(2,1)S(1)} all-to-all(bf16[16,264,128]{2,1,0:T(8,128)(2,1)S(1)} %shard_map.99), channel_id=1, replica_groups=mesh['role'=4,'zhi'=2,'x'=4,'y'=4,'core'=2] {'x','y'}, dimensions={0} | all-to-all | bytes 2162688 | tf_op jit(solution)/shard_map/all_to_all | solution.py:356
  68.7 0.3 shard_map.100
  69.0 10.4 %all_to_all.22.parts_ref = bf16[8,48,128]{2,1,0:T(8,128)(2,1)S(1)} all-to-all(bf16[8,48,128]{2,1,0:T(8,128)(2,1)S(1)} %shard_map.100), channel_id=1, replica_groups=mesh['role'=4,'zhi'=2,'x'=4,'y'=4,'core'=2] {'role','zhi'}, dimensions={0} | all-to-all | bytes 196608 | tf_op jit(solution)/shard_map/all_to_all | solution.py:358
  79.4 0.8 shard_map.101
Async XLA Ops:
  0.6 25.6 %collective-permute-start = (bf16[2,2,80,7168]{3,2,1,0:T(8,128)(2,1)}, bf16[2,2,80,7168]{3,2,1,0:T(8,128)(2,1)}, u32[]{:S(2)}, u32[]{:S(2)}) collective-permute-start(bf16[2,2,80,7168]{3,2,1,0:T(8,128)(2,1)} %bitcast.6), channel_id=1, source_target_pairs={{0,1},{1,0},{2,3},{3,2},{4,5},{5,4},{6,7},{7,6},{8,9},{9,8},{10,11... | collective-permute-start | bytes 13762568 | tf_op jit(solution)/shard_map/ppermute | solution.py:320
  0.7 25.4 %collective-permute-start.1 = (bf16[2,80,7168]{2,1,0:T(8,128)(2,1)}, bf16[2,80,7168]{2,1,0:T(8,128)(2,1)}, u32[]{:S(2)}, u32[]{:S(2)}) collective-permute-start(bf16[2,80,7168]{2,1,0:T(8,128)(2,1)} %down_hbm.1), channel_id=1, source_target_pairs={{0,1},{1,0},{2,3},{3,2},{4,5},{5,4},{6,7},{7,6},{8,9},{9,8},{10,11... | collective-permute-start | bytes 6881288 | tf_op jit(solution)/shard_map/ppermute | solution.py:320
  19.1 21.9 %all-to-all-start.1 = ((bf16[16,224,128]{2,1,0:T(8,128)(2,1)}), bf16[16,224,128]{2,1,0:T(8,128)(2,1)S(1)}, u32[]{:S(2)}, u32[]{:S(2)}) async-start(bf16[16,224,128]{2,1,0:T(8,128)(2,1)} %get-tuple-element.10.after_ref), calls=%async_computation.1 | async-start | bytes 1835008 | tf_op jit(solution)/shard_map/all_to_all | solution.py:315
  37.1 9.1 %collective-permute-start.3 = (bf16[32,8,384]{2,1,0:T(8,128)(2,1)}, bf16[32,8,384]{2,1,0:T(8,128)(2,1)S(1)}, u32[]{:S(2)}, u32[]{:S(2)}) collective-permute-start(bf16[32,8,384]{2,1,0:T(8,128)(2,1)} %get-tuple-element.17), channel_id=1, source_target_pairs={{0,1},{1,0},{2,3},{3,2},{4,5},{5,4},{6,7},{7,6},{8,9},{9,8},{10,11... | collective-permute-start | bytes 589832 | tf_op jit(solution)/shard_map/ppermute | solution.py:354
  41.0 2.3 %copy-start = (bf16[640,3584]{1,0:T(8,128)(2,1)S(1)}, bf16[640,3584]{1,0:T(8,128)(2,1)}, u32[]{:S(2)}) copy-start(bf16[640,3584]{1,0:T(8,128)(2,1)} %get-tuple-element.11.gate_ref) | copy-start | bytes 13762564
  43.3 2.8 %copy-start.1 = (bf16[320,3584]{1,0:T(8,128)(2,1)S(1)}, bf16[320,3584]{1,0:T(8,128)(2,1)}, u32[]{:S(2)}) copy-start(bf16[320,3584]{1,0:T(8,128)(2,1)} %get-tuple-element.15.down_ref) | copy-start | bytes 6881284
  43.3 2.8 %copy-start.2 = (bf16[32,8,384]{2,1,0:T(8,128)(2,1)S(1)}, bf16[32,8,384]{2,1,0:T(8,128)(2,1)}, u32[]{:S(2)}) copy-start(bf16[32,8,384]{2,1,0:T(8,128)(2,1)} %get-tuple-element.16.attended_ref) | copy-start | bytes 589828
  44.7 1.5 %collective-permute-start.2 = (bf16[640,128]{1,0:T(8,128)(2,1)S(1)}, bf16[640,128]{1,0:T(8,128)(2,1)S(1)}, u32[]{:S(2)}, u32[]{:S(2)}) collective-permute-start(bf16[640,128]{1,0:T(8,128)(2,1)S(1)} %get-tuple-element.13), channel_id=1, source_target_pairs={{0,1},{1,0},{2,3},{3,2},{4,5},{5,4},{6,7},{7,6},{8,9},{9,8},{10,11... | collective-permute-start | bytes 491528 | tf_op jit(solution)/shard_map/ppermute | solution.py:354

commit v6 on v5

--- a/solution.py
+++ b/solution.py
@@ -153,9 +153,9 @@
     loads = [
         pltpu.make_async_copy(source, in_ref.at[i], in_sems.at[i]) for i, source in enumerate(sources)
     ]
+    q_load.wait()
     for load in loads[:4]:
         load.start()
-    q_load.wait()
     for load in cache_loads:
         load.wait()
     for load in loads[4:]:

time: 80.6 us -> 80.3 us (level)
  waiting for transfers between devices: 5.22 us -> 6.25 us
  Pallas kernels: 16.8 us -> 15.8 us
    pallas_call x7, Pallas kernels: 16.8 us -> 15.8 us  [call(): pl.pallas_call(kernel, out_shape=out_shape, in_specs=specs or [VMEM] * le...]
    all_to_all x1, waiting for transfers between devices: 3.83 us -> 4.86 us  [shards(): gathered = lax.all_to_all(packed, ('x', 'y'), 0, 0, tiled=True)]
  transfers between devices with their start and end apart: 5 -> 5, of which waited for: 2 -> 2; matrix products, arithmetic and copies ran while one was open for 0% -> 0% of each run, Pallas kernels for 18% -> 17%
where the time goes in v6:
time: 80.3 us; the launch traced here: 79.9 us
  blocking collectives  47 us (59%)
  Pallas kernels  15.8 us (20%)
  starting transfers between devices  7.81 us (10%)
  waiting for transfers between devices  6.25 us (8%)
  local copies, waits for them, and re-layouts  2.31 us (3%)
    all_to_all x1, blocking collectives, shards(): spread = lax.all_to_all(half, ('x', 'y'), 0, 0, tiled=True)  21.3 us
    pallas_call x7, Pallas kernels, call(): pl.pallas_call(kernel, out_shape=out_shape, in_specs=specs or [VMEM] * le...  15.8 us
    all_to_all x1, blocking collectives, shards(): rows = lax.all_to_all(message, ('role', 'zhi'), 0, 0, tiled=True)  15.4 us
    all_to_all x1, blocking collectives, shards(): ends = lax.all_to_all(partial, ('role', 'zhi'), 0, 0, tiled=True)  10.3 us
    all_to_all x1, starting transfers between devices, shards(): gathered = lax.all_to_all(packed, ('x', 'y'), 0, 0, tiled=True)  7.03 us
    all_to_all x1, waiting for transfers between devices, shards(): gathered = lax.all_to_all(packed, ('x', 'y'), 0, 0, tiled=True)  4.86 us
    unnamed x6, local copies, waits for them, and re-layouts  2.31 us
  transfers between devices with their start and end apart: 5, of which 2 were waited for; matrix products, arithmetic and copies ran while one was open for 0% of the time, Pallas kernels for 17%

profile of v6, /device:TPU:32, one launch (start us, length us, event | category | flops | bytes accessed | tf_op | source)
XLA Modules:
  0.0 79.9 jit_solution(17787150547633407170)
XLA Ops:
  0.6 0.1 collective-permute-start
  0.7 0.5 collective-permute-start.1
  1.2 1.4 %shard_map.95 = bf16[8,32,128]{2,1,0:T(8,128)(2,1)} custom-call(bf16[32,112]{1,0:T(8,128)(2,1)} %x_hbm.1, s32[3,32]{1,0:T(4,128)} %bitcast.9, f32[3,32]{1,0:T(4,128)} %bitcast.10), custom_call_target="tpu_custom_call" | custom-call | tf_op jit(solution)/shard_map/pallas_call | solution.py:24
  2.7 15.4 %all_to_all.20.rows_ref = bf16[8,32,128]{2,1,0:T(8,128)(2,1)S(1)} all-to-all(bf16[8,32,128]{2,1,0:T(8,128)(2,1)} %shard_map.95), channel_id=1, replica_groups=mesh['role'=4,'zhi'=2,'x'=4,'y'=4,'core'=2] {'role','zhi'}, dimensions={0} | all-to-all | bytes 131072 | tf_op jit(solution)/shard_map/all_to_all | solution.py:313
  18.1 1.1 %shard_map.96 = (bf16[16,224,128]{2,1,0:T(8,128)(2,1)}, f32[8,128]{1,0:T(8,128)S(1)}) custom-call(bf16[8,32,128]{2,1,0:T(8,128)(2,1)S(1)} %all_to_all.20.rows_ref), custom_call_target="tpu_custom_call" | custom-call | tf_op jit(solution)/shard_map/pallas_call | solution.py:24
  19.1 7.0 %all-to-all-start.1 = ((bf16[16,224,128]{2,1,0:T(8,128)(2,1)}), bf16[16,224,128]{2,1,0:T(8,128)(2,1)S(1)}, u32[]{:S(2)}, u32[]{:S(2)}) async-start(bf16[16,224,128]{2,1,0:T(8,128)(2,1)} %get-tuple-element.10.after_ref), calls=%async_computation.1 | async-start | bytes 1835008 | tf_op jit(solution)/shard_map/all_to_all | solution.py:315
  26.2 0.0 collective-permute-done.1.got_down_hbm
  26.2 0.0 collective-permute-done.got_gate_hbm
  26.2 9.8 %shard_map.97 = (bf16[32,8,384]{2,1,0:T(8,128)(2,1)}, bf16[32,8,384]{2,1,0:T(8,128)(2,1)}, bf16[640,3584]{1,0:T(8,128)(2,1)}, bf16[320,3584]{1,0:T(8,128)(2,1)}) custom-call(s32[8]{0:T(128)} %seq_ref.1, bf16[32,2,8,256]{3,2,1,0:T(8,128)(2,1)} %bitcast.8, bf16[2,1024,512]{2,1,0:T(8,128)(2,1)} %cache_hbm.1, bf16[2,2,80,7168]{3,2,1,0:T(8,128)(2,1)} %bitcast.7, ...), custom_call_target="tpu_custom_call" | custom-call | flops 2147483648 | bytes 25165824 | tf_op jit(solution)/shard_map/pallas_call | solution.py:24
  36.0 0.1 collective-permute-start.3
  36.1 4.9 %all-to-all-done.1.rows_ref = bf16[16,224,128]{2,1,0:T(8,128)(2,1)S(1)} async-done(((bf16[16,224,128]{2,1,0:T(8,128)(2,1)}), bf16[16,224,128]{2,1,0:T(8,128)(2,1)S(1)}, u32[]{:S(2)}, u32[]{:S(2)}) %all-to-all-start.1) | async-done | bytes 917536 | tf_op jit(solution)/shard_map/all_to_all | solution.py:315
  41.0 0.0 copy-start
  41.0 2.3 %copy-done = bf16[640,3584]{1,0:T(8,128)(2,1)S(1)} copy-done((bf16[640,3584]{1,0:T(8,128)(2,1)S(1)}, bf16[640,3584]{1,0:T(8,128)(2,1)}, u32[]{:S(2)}) %copy-start) | copy-done | bytes 4587544
  43.3 0.0 copy-start.1
  43.3 0.0 copy-start.2
  43.3 1.3 %shard_map.98 = (f32[640,128]{1,0:T(8,128)S(1)}, bf16[640,128]{1,0:T(8,128)(2,1)S(1)}) custom-call(bf16[16,224,128]{2,1,0:T(8,128)(2,1)S(1)} %all-to-all-done.1.rows_ref, bf16[640,3584]{1,0:T(8,128)(2,1)S(1)} %copy-done), custom_call_target="tpu_custom_call" | custom-call | tf_op jit(solution)/shard_map/pallas_call | solution.py:24
  44.7 0.1 collective-permute-start.2
  44.8 1.4 %collective-permute-done.2.theirs_ref = bf16[640,128]{1,0:T(8,128)(2,1)S(1)} collective-permute-done((bf16[640,128]{1,0:T(8,128)(2,1)S(1)}, bf16[640,128]{1,0:T(8,128)(2,1)S(1)}, u32[]{:S(2)}, u32[]{:S(2)}) %collective-permute-start.2) | collective-permute-done | bytes 163872 | tf_op jit(solution)/shard_map/ppermute | solution.py:354
  46.1 0.0 collective-permute-done.3.their_attended_ref
  46.1 0.0 copy-done.1
  46.1 0.0 copy-done.2
  46.1 1.0 %shard_map.99 = bf16[16,264,128]{2,1,0:T(8,128)(2,1)S(1)} custom-call(f32[640,128]{1,0:T(8,128)S(1)} %get-tuple-element.12.mine_ref, bf16[640,128]{1,0:T(8,128)(2,1)S(1)} %collective-permute-done.2.theirs_ref, f32[8,128]{1,0:T(8,128)S(1)} %get-tuple-element.14.weight_ref, bf16[320,3584]{1,0:T(8,128)(2,1)S(1)} %copy-done.1, ...), custom_call_target="tpu_custom_call" | custom-call | tf_op jit(solution)/shard_map/pallas_call | solution.py:24
  47.2 21.3 %all_to_all.21.parts_ref = bf16[16,264,128]{2,1,0:T(8,128)(2,1)S(1)} all-to-all(bf16[16,264,128]{2,1,0:T(8,128)(2,1)S(1)} %shard_map.99), channel_id=1, replica_groups=mesh['role'=4,'zhi'=2,'x'=4,'y'=4,'core'=2] {'x','y'}, dimensions={0} | all-to-all | bytes 2162688 | tf_op jit(solution)/shard_map/all_to_all | solution.py:356
  68.5 0.3 shard_map.100
  68.8 10.3 %all_to_all.22.parts_ref = bf16[8,48,128]{2,1,0:T(8,128)(2,1)S(1)} all-to-all(bf16[8,48,128]{2,1,0:T(8,128)(2,1)S(1)} %shard_map.100), channel_id=1, replica_groups=mesh['role'=4,'zhi'=2,'x'=4,'y'=4,'core'=2] {'role','zhi'}, dimensions={0} | all-to-all | bytes 196608 | tf_op jit(solution)/shard_map/all_to_all | solution.py:358
  79.1 0.8 shard_map.101
Async XLA Ops:
  0.6 25.6 %collective-permute-start = (bf16[2,2,80,7168]{3,2,1,0:T(8,128)(2,1)}, bf16[2,2,80,7168]{3,2,1,0:T(8,128)(2,1)}, u32[]{:S(2)}, u32[]{:S(2)}) collective-permute-start(bf16[2,2,80,7168]{3,2,1,0:T(8,128)(2,1)} %bitcast.6), channel_id=1, source_target_pairs={{0,1},{1,0},{2,3},{3,2},{4,5},{5,4},{6,7},{7,6},{8,9},{9,8},{10,11... | collective-permute-start | bytes 13762568 | tf_op jit(solution)/shard_map/ppermute | solution.py:320
  0.7 25.4 %collective-permute-start.1 = (bf16[2,80,7168]{2,1,0:T(8,128)(2,1)}, bf16[2,80,7168]{2,1,0:T(8,128)(2,1)}, u32[]{:S(2)}, u32[]{:S(2)}) collective-permute-start(bf16[2,80,7168]{2,1,0:T(8,128)(2,1)} %down_hbm.1), channel_id=1, source_target_pairs={{0,1},{1,0},{2,3},{3,2},{4,5},{5,4},{6,7},{7,6},{8,9},{9,8},{10,11... | collective-permute-start | bytes 6881288 | tf_op jit(solution)/shard_map/ppermute | solution.py:320
  19.1 21.9 %all-to-all-start.1 = ((bf16[16,224,128]{2,1,0:T(8,128)(2,1)}), bf16[16,224,128]{2,1,0:T(8,128)(2,1)S(1)}, u32[]{:S(2)}, u32[]{:S(2)}) async-start(bf16[16,224,128]{2,1,0:T(8,128)(2,1)} %get-tuple-element.10.after_ref), calls=%async_computation.1 | async-start | bytes 1835008 | tf_op jit(solution)/shard_map/all_to_all | solution.py:315
  36.0 10.1 %collective-permute-start.3 = (bf16[32,8,384]{2,1,0:T(8,128)(2,1)}, bf16[32,8,384]{2,1,0:T(8,128)(2,1)S(1)}, u32[]{:S(2)}, u32[]{:S(2)}) collective-permute-start(bf16[32,8,384]{2,1,0:T(8,128)(2,1)} %get-tuple-element.17), channel_id=1, source_target_pairs={{0,1},{1,0},{2,3},{3,2},{4,5},{5,4},{6,7},{7,6},{8,9},{9,8},{10,11... | collective-permute-start | bytes 589832 | tf_op jit(solution)/shard_map/ppermute | solution.py:354
  41.0 2.3 %copy-start = (bf16[640,3584]{1,0:T(8,128)(2,1)S(1)}, bf16[640,3584]{1,0:T(8,128)(2,1)}, u32[]{:S(2)}) copy-start(bf16[640,3584]{1,0:T(8,128)(2,1)} %get-tuple-element.11.gate_ref) | copy-start | bytes 13762564
  43.3 2.8 %copy-start.1 = (bf16[320,3584]{1,0:T(8,128)(2,1)S(1)}, bf16[320,3584]{1,0:T(8,128)(2,1)}, u32[]{:S(2)}) copy-start(bf16[320,3584]{1,0:T(8,128)(2,1)} %get-tuple-element.15.down_ref) | copy-start | bytes 6881284
  43.3 2.8 %copy-start.2 = (bf16[32,8,384]{2,1,0:T(8,128)(2,1)S(1)}, bf16[32,8,384]{2,1,0:T(8,128)(2,1)}, u32[]{:S(2)}) copy-start(bf16[32,8,384]{2,1,0:T(8,128)(2,1)} %get-tuple-element.16.attended_ref) | copy-start | bytes 589828
  44.7 1.5 %collective-permute-start.2 = (bf16[640,128]{1,0:T(8,128)(2,1)S(1)}, bf16[640,128]{1,0:T(8,128)(2,1)S(1)}, u32[]{:S(2)}, u32[]{:S(2)}) collective-permute-start(bf16[640,128]{1,0:T(8,128)(2,1)S(1)} %get-tuple-element.13), channel_id=1, source_target_pairs={{0,1},{1,0},{2,3},{3,2},{4,5},{5,4},{6,7},{7,6},{8,9},{9,8},{10,11... | collective-permute-start | bytes 491528 | tf_op jit(solution)/shard_map/ppermute | solution.py:354
